TPU v7x, 256 devices: a whole 4x4x8 slice. The times are simulated.
256 devices in a mesh: group: 16 (over z_hi, y), head: 16 (over x, z_lo, core).
Axes of the slice: x: 4, y: 4, z: 8 (z_hi: 4, z_lo: 2; z = z_hi * 2 + z_lo), core: 2. Of those that a mesh axis runs over, the one named last changes fastest.
Arguments:
- old_pool: bfloat16 [768, 256, 576], P('group', 'head'), may hold values from -6 to 6
- mig_source: int32 [16, 16, 1], replicated, may hold values from 0 to 15; in each aligned block of 16 rows (0 to 15, 16 to 31, ..., all dimensions but the last counted through in order) at most 2 rows name the same one
- mig_page: int32 [16, 16], replicated, may hold values from 0 to 47
- page_table: int32 [16, 64], P('group'), may hold values from 0 to 63, each once within a row
- lengths: int32 [256], P('group'), may hold values from 1 to 1024
- queries: bfloat16 [256, 2, 128, 576], P('group', None, 'head'), may hold values from -300 to 300
- new_latent: bfloat16 [256, 2, 576], P('group'), may hold values from -6 to 6
- w_uv: bfloat16 [128, 512, 128], P('head'), may hold values from -0.25 to 0.25
- w_out: bfloat16 [16384, 4096], P(None, 'head'), may hold values from -0.046875 to 0.046875
Outputs:
- projected: bfloat16 [256, 2, 4096], P('group', None, 'head')
Inputs may be any that keep to these rules, and one draw needn't show every extreme that they name: `mig_source`: among the 16 slots of one destination group no source group is named more than 2 times; in some destination group one source is named exactly 2 times. `page_table`: each row is a permutation of the 64 pages of its group's pool.
All inputs are finite; a program needn't handle non-finite values.
Results may differ from a plain program's by a relative error of at most 0.015.
Values may be sent and summed in bfloat16 or wider, within the bound.
A program may use at most 128 MiB of HBM per device.

v0:
```python
import jax
import jax.numpy as jnp
from jax import lax
from jax.sharding import PartitionSpec as P

KVR = 512
ROPE = 64
VD = 128
PAGE = 256
PAGES_SEQ = 4
CAP = 2
LAT = 576


masked_score = -1e30


def partial_attention(query, key_rows, visible, scale):
    scores = (
        jnp.einsum("sthc,slc->sthl", query, key_rows, preferred_element_type=jnp.float32) * scale
    )
    shown = visible[:, None, None, :]
    highest = jnp.max(jnp.where(shown, scores, masked_score), axis=3)
    weights = jnp.where(shown, jnp.exp(scores - highest[..., None]), 0.0)
    totals = jnp.sum(weights, axis=3)
    weighted = jnp.einsum(
        "sthl,slc->sthc",
        weights.astype(jnp.bfloat16),
        key_rows[:, :, :KVR],
        preferred_element_type=jnp.float32,
    )
    return (highest, totals, weighted)


def blend(first, second):
    top = jnp.maximum(first[0], second[0])
    first_factor = jnp.exp(first[0] - top)
    second_factor = jnp.exp(second[0] - top)
    totals = first[1] * first_factor + second[1] * second_factor
    weighted = first[2] * first_factor[..., None] + second[2] * second_factor[..., None]
    return (top, totals, weighted)


def shards(old_pool, mig_source, mig_page, page_table, lengths, queries, new_latent, w_uv, w_out):
    groups = lax.axis_size("group")
    my_group = lax.axis_index("group")
    page_rows = old_pool.shape[1]
    source = mig_source[:, :, 0]
    migrate = source.shape[1]
    order = jnp.arange(migrate)
    same_source = source[:, :, None] == source[:, None, :]
    earlier = order[None, None, :] < order[None, :, None]
    slot_rank = jnp.sum(same_source & earlier, axis=2)
    slots = jnp.arange(CAP)
    chosen = (source[:, None, :] == my_group) & (slot_rank[:, None, :] == slots[None, :, None])
    picked = jnp.sum(jnp.where(chosen, mig_page[:, None, :], 0), axis=2)
    outgoing = jnp.take(old_pool, picked.reshape(-1), axis=0).reshape(groups, CAP, page_rows, LAT)
    arrived = lax.all_to_all(outgoing, "group", split_axis=0, concat_axis=0, tiled=True)
    wanted = lax.dynamic_index_in_dim(source, my_group, 0, keepdims=False)
    wanted_rank = lax.dynamic_index_in_dim(slot_rank, my_group, 0, keepdims=False)
    incoming = jnp.take(
        arrived.reshape(groups * CAP, page_rows, LAT), wanted * CAP + wanted_rank, axis=0
    )
    fresh_pool = jnp.concatenate([old_pool, incoming], axis=0)
    seq_count = queries.shape[0]
    page_map = page_table[0].reshape(seq_count, PAGES_SEQ)
    scale = (VD + ROPE) ** (-0.5)
    new_scores = (
        jnp.einsum("sthc,suc->sthu", queries, new_latent, preferred_element_type=jnp.float32)
        * scale
    )
    causal = (jnp.arange(2)[None, :] <= jnp.arange(2)[:, None])[None, :, None, :]
    new_peak = jnp.max(jnp.where(causal, new_scores, masked_score), axis=3)
    new_weights = jnp.where(causal, jnp.exp(new_scores - new_peak[..., None]), 0.0)
    new_total = jnp.sum(new_weights, axis=3)
    new_sums = jnp.einsum(
        "sthu,suc->sthc",
        new_weights.astype(jnp.bfloat16),
        new_latent[:, :, :KVR],
        preferred_element_type=jnp.float32,
    )
    shard_rows = lax.all_gather(fresh_pool, "head", axis=1, tiled=True)
    width = shard_rows.shape[1]
    key_rows = jnp.take(shard_rows, page_map, axis=0).reshape(seq_count, PAGES_SEQ * width, LAT)
    positions = (jnp.arange(PAGES_SEQ)[:, None] * PAGE + jnp.arange(width)[None, :]).reshape(-1)
    visible = positions[None, :] < lengths[:, None]
    highest, totals, weighted = blend(
        (new_peak, new_total, new_sums), partial_attention(queries, key_rows, visible, scale)
    )
    latent = (weighted / totals[..., None]).astype(jnp.bfloat16)
    head_values = jnp.einsum(
        "sthc,hcv->sthv", latent, w_uv, preferred_element_type=jnp.float32
    ).astype(jnp.bfloat16)
    flattened = head_values.reshape(seq_count * 2, head_values.shape[2] * head_values.shape[3])
    result = jnp.dot(
        lax.all_gather(flattened, "head", axis=1, tiled=True),
        w_out,
        preferred_element_type=jnp.float32,
    )
    return result.reshape(seq_count, 2, w_out.shape[1]).astype(jnp.bfloat16)


def solution(mesh):
    return jax.shard_map(
        shards,
        mesh=mesh,
        in_specs=(
            P("group", "head", None),
            P(),
            P(),
            P("group", None),
            P("group"),
            P("group", None, "head", None),
            P("group", None, None),
            P("head", None, None),
            P(None, "head"),
        ),
        out_specs=P("group", None, "head"),
        check_vma=False,
    )
```

profile of v0, /device:TPU:1, one launch (start us, length us, event | category | flops | bytes accessed | tf_op | source)
XLA Modules:
  0.0 261.3 jit_solution(7490023704791885292)
XLA Ops:
  6.5 0.0 copy-start
  6.5 0.8 broadcast_compare_fusion.1
  7.3 1.2 convert_reduce_fusion
  8.5 0.8 select_reduce_fusion.2
  9.4 0.1 copy.20
  9.4 0.1 reshape.233
  9.6 0.1 copy.19
  9.7 1.9 gather_fusion
  11.5 1.0 broadcast_select_fusion
  12.5 11.7 %all-to-all-start = ((bf16[16,2,16,576]{3,2,1,0:T(8,128)(2,1)}), bf16[16,2,16,576]{3,2,1,0:T(8,128)(2,1)S(1)}, u32[]{:S(2)}, u32[]{:S(2)}) async-start(bf16[16,2,16,576]{3,2,1,0:T(8,128)(2,1)} %broadcast_select_fusion), calls=%async_computation | async-start | bytes 1310720 | tf_op jit(solution)/shard_map/all_to_all | solution.py:58
  24.3 0.0 all-gather.3.cloned.1.call-start
  24.3 0.7 fusion.25
  25.0 0.7 compare_and_fusion.2
  25.7 16.2 %all-to-all-done = bf16[16,2,16,576]{3,2,1,0:T(8,128)(2,1)S(1)} async-done(((bf16[16,2,16,576]{3,2,1,0:T(8,128)(2,1)}), bf16[16,2,16,576]{3,2,1,0:T(8,128)(2,1)S(1)}, u32[]{:S(2)}, u32[]{:S(2)}) %all-to-all-start) | async-done | bytes 589856 | tf_op jit(solution)/shard_map/all_to_all | solution.py:58
  41.9 0.6 gather_fusion.1
  42.5 0.1 broadcast_select_fusion.1
  42.6 2.4 pad_maximum_fusion
  45.1 0.0 all-gather.3.cloned.1.call-update
  45.1 0.0 all-gather.5.cloned.1.call-start
  45.1 0.7 reshape_squeeze.6
  45.9 0.1 reshape.254
  46.0 0.5 broadcast.189
  46.5 1.3 reduce.6
  47.8 0.1 reshape_squeeze.5
  47.9 0.1 broadcast_in_dim.105
  48.0 0.1 add_bitcast_fusion
  48.1 2.0 select_reduce_fusion.1
  50.1 0.1 fusion.23
  50.2 0.7 broadcast_compare_fusion
  51.0 108.2 %all-gather.3.cloned.1.call-done = bf16[64,256,576]{2,1,0:T(8,128)(2,1)} async-done(((bf16[64,16,576]{2,1,0:T(8,128)(2,1)}), bf16[64,256,576]{2,1,0:T(8,128)(2,1)}) %all-gather.3.cloned.1.call-update) | async-done | bytes 18874384 | tf_op jit(solution)/shard_map/all_gather | solution.py:82
  159.2 16.3 %gather_fusion.2 = bf16[64,256,576]{2,1,0:T(8,128)(2,1)} fusion(bf16[64,256,576]{2,1,0:T(8,128)(2,1)} %all-gather.3.cloned.1.call-done, s32[1024]{0:T(1024)S(1)} %pad_clamp_fusion), kind=kCustom, calls=%fused_computation.2 | custom fusion | bytes 37748992 | tf_op jit(solution)/shard_map/jit(_take)/gather | solution.py:84
  175.5 0.0 copy-start.1
  175.5 18.4 %bitcast_select_fusion = bf16[16,1024,576]{2,1,0:T(8,128)(2,1)} fusion(pred[16,1024]{1,0:T(8,128)(4,1)S(1)} %bitcast.94, bf16[16,1024,576]{2,1,0:T(8,128)(2,1)} %bitcast.85), kind=kLoop, calls=%fused_computation.5 | loop fusion | flops 9437184 | bytes 37765120 | tf_op jit(solution)/shard_map/jit(_take)/select_n | solution.py:84
  193.9 0.0 copy-done.1
  193.9 9.9 %select_reduce_fusion = (f32[16,2,8]{2,1,0:T(2,128)S(1)}, f32[16,1024,2,8]{1,3,2,0:T(8,128)S(1)}) fusion(pred[16,1024]{1,0:T(8,128)(4,1)S(1)} %broadcast_compare_fusion, bf16[16,2,8,576]{3,2,1,0:T(8,128)(2,1)S(1)} %copy-done.1, bf16[16,1024,576]{2,1,0:T(8,128)(2,1)} %bitcast_select_fusion), kind=kOutput, calls=%fused_computation.23 | convolution fusion | flops 302776064 | bytes 20235264 | tf_op jit(solution)/shard_map/sthc,slc->sthl/dot_general | solution.py:20
  203.8 0.0 copy-start.2
  203.8 0.4 bitcast_reduce_fusion
  204.2 7.0 %fusion.8 = f32[16,2,8,512]{3,2,1,0:T(8,128)S(1)} fusion(bf16[16,1024,576]{2,1,0:T(8,128)(2,1)} %bitcast_select_fusion, f32[16,1024,2,8]{1,3,2,0:T(8,128)S(1)} %get-tuple-element.9, f32[16,2,8]{2,1,0:T(2,128)S(1)} %get-tuple-element.8, pred[16,1024]{1,0:T(8,128)(4,1)S(1)} %broadcast_compare_fusion, f32[16,2,8]{2,1,0:T(2,128)S(1)} %bitcast.100), kind=kOutput, calls=%fused_computation.13 | convolution fusion | flops 269352960 | bytes 18368512 | tf_op jit(solution)/shard_map/sthl,slc->sthc/dot_general | solution.py:26
  211.2 0.0 copy-done.2
  211.2 0.4 fusion.9
  211.6 0.0 copy-done
  211.7 0.4 fusion.10
  212.1 0.6 copy.37
  212.7 0.0 all-gather.5.cloned.1.call-update
  212.7 35.9 %all-gather.5.cloned.1.call-done = bf16[32,16384]{1,0:T(8,128)(2,1)} async-done(((bf16[32,1024]{1,0:T(8,128)(2,1)}), bf16[32,16384]{1,0:T(8,128)(2,1)}) %all-gather.5.cloned.1.call-update) | async-done | bytes 1048592 | tf_op jit(solution)/shard_map/all_gather | solution.py:96
  248.6 5.3 %convolution_convert_fusion.1 = bf16[32,256]{1,0:T(8,128)(2,1)S(1)} fusion(bf16[32,16384]{1,0:T(8,128)(2,1)} %all-gather.5.cloned.1.call-done, bf16[16384,256]{1,0:T(8,128)(2,1)} %param.17), kind=kOutput, calls=%fused_computation.18 | convolution fusion | flops 268443648 | bytes 9453568 | tf_op jit(solution)/shard_map/dot_general | solution.py:95
  253.8 0.6 convert_element_type.31
  (14 shorter events, 0.1 us)
Async XLA Ops:
  6.5 205.1 %copy-start = (bf16[8,512,128]{2,1,0:T(8,128)(2,1)S(1)}, bf16[8,512,128]{2,1,0:T(8,128)(2,1)}, u32[]{:S(2)}) copy-start(bf16[8,512,128]{2,1,0:T(8,128)(2,1)} %param.16) | copy-start | bytes 3145732
  12.5 29.4 %all-to-all-start = ((bf16[16,2,16,576]{3,2,1,0:T(8,128)(2,1)}), bf16[16,2,16,576]{3,2,1,0:T(8,128)(2,1)S(1)}, u32[]{:S(2)}, u32[]{:S(2)}) async-start(bf16[16,2,16,576]{3,2,1,0:T(8,128)(2,1)} %broadcast_select_fusion), calls=%async_computation | async-start | bytes 1310720 | tf_op jit(solution)/shard_map/all_to_all | solution.py:58
  24.3 134.9 %all-gather.3.cloned.1.call-start = ((), (), s32[]{:S(2)}) async-start(), calls=%async_computation.1 | async-start | bytes 22282240 | tf_op jit(solution)/shard_map/all_gather | solution.py:82
  45.1 203.5 %all-gather.5.cloned.1.call-start = ((), (), s32[]{:S(2)}) async-start(), calls=%async_computation.2 | async-start | bytes 1114112 | tf_op jit(solution)/shard_map/all_gather | solution.py:96
  175.5 18.4 %copy-start.1 = (bf16[16,2,8,576]{3,2,1,0:T(8,128)(2,1)S(1)}, bf16[16,2,8,576]{3,2,1,0:T(8,128)(2,1)}, u32[]{:S(2)}) copy-start(bf16[16,2,8,576]{3,2,1,0:T(8,128)(2,1)} %param.14) | copy-start | bytes 884740
  203.8 7.5 %copy-start.2 = (bf16[16,2,576]{2,1,0:T(2,128)(2,1)S(1)}, bf16[16,2,576]{2,1,0:T(2,128)(2,1)}, u32[]{:S(2)}) copy-start(bf16[16,2,576]{2,1,0:T(2,128)(2,1)} %param.15) | copy-start | bytes 110596
Sparse Core Ops, SparseCore 0:
  45.2 113.9 all-gather.2
  212.9 35.6 all-gather.4
where the time goes:
time: 262 us; the launch traced here: 261 us
  waiting for transfers between devices  160 us (61%)
  other arithmetic  28.8 us (11%)
  matrix products  24.9 us (10%)
  local copies, waits for them, and re-layouts  21.9 us (8%)
  between operations  13.6 us (5%)
  starting transfers between devices  11.8 us (5%)
    all_gather x1, waiting for transfers between devices, shards(): shard_rows = lax.all_gather(fresh_pool, 'head', axis=1, tiled=True)  108 us
    all_gather x1, waiting for transfers between devices, shards(): lax.all_gather(flattened, 'head', axis=1, tiled=True)  35.9 us
    select_n x2, other arithmetic, shards(): jnp.take(shard_rows, page_map, axis=0)  18.4 us
    gather x1, local copies, waits for them, and re-layouts, shards(): jnp.take(shard_rows, page_map, axis=0)  16.3 us
    all_to_all x1, waiting for transfers between devices, shards(): lax.all_to_all(outgoing, 'group', split_axis=0, concat_axis=0, tiled=True)  16.2 us
    all_to_all x1, starting transfers between devices, shards(): lax.all_to_all(outgoing, 'group', split_axis=0, concat_axis=0, tiled=True)  11.7 us
    dot_general x1, matrix products, partial_attention(): jnp.einsum('sthc,slc->sthl', query, key_rows, preferred_element_type=jnp....  9.88 us
    dot_general x1, matrix products, partial_attention(): jnp.einsum('sthl,slc->sthc', weights.astype(jnp.bfloat16), key_rows[:, :,...  7.04 us
  transfers between devices with their start and end apart: 3, of which 3 were waited for; matrix products, arithmetic and copies ran while one was open for 3% of the time, Pallas kernels for 0%

commit v1 on v0

v1 whole, which is shorter than its diff:
```python
import functools

import jax
import jax.numpy as jnp
from jax import lax
from jax.experimental import pallas as pl
from jax.experimental.pallas import tpu as pltpu
from jax.sharding import PartitionSpec as P

KVR = 512
ROPE = 64
VD = 128
CAP = 2
MESH = pl.DeviceIdType.MESH
HIDDEN = -1e30


def kernel(
    dims,
    source_ref,
    page_ref,
    table_ref,
    length_ref,
    pool_hbm,
    query_hbm,
    new_ref,
    w_uv_hbm,
    w_out_hbm,
    out_ref,
    pool,
    pages,
    mig_out,
    keys,
    kv_out,
    queries,
    scores,
    lat_out,
    lat_in,
    values,
    w_uv,
    w_out,
    place,
    mig_send,
    mig_recv,
    q_send,
    q_recv,
    kv_send,
    kv_recv,
    lat_send,
    lat_recv,
    hv_send,
    hv_recv,
    local_sem,
):
    groups, heads, own, slots, rows, migrate, heads_each, page_len = dims
    my_group = lax.axis_index("group")
    me = lax.axis_index("head")
    lat = pool_hbm.shape[2]
    width = slots * rows
    lanes = heads * width

    pool_copy = pltpu.make_async_copy(pool_hbm, pool, local_sem.at[0])
    pool_copy.start()
    page_copy = pltpu.make_async_copy(pool_hbm, pages.at[pl.ds(0, own)], local_sem.at[4])
    page_copy.start()

    barrier = pltpu.get_barrier_semaphore()
    for d in range(1, groups):
        to = lax.rem(my_group + d, groups)
        pl.semaphore_signal(barrier, inc=1, device_id=(to, me), device_id_type=MESH)
    for d in range(1, heads):
        to = lax.rem(me + d, heads)
        pl.semaphore_signal(barrier, inc=1, device_id=(my_group, to), device_id_type=MESH)

    query_copy = pltpu.make_async_copy(query_hbm.at[me], queries.at[me], local_sem.at[1])
    query_copy.start()
    uv_copy = pltpu.make_async_copy(w_uv_hbm, w_uv, local_sem.at[2])
    uv_copy.start()
    out_copy = pltpu.make_async_copy(w_out_hbm, w_out, local_sem.at[3])
    out_copy.start()

    def wanted_by(group):
        first = jnp.int32(0)
        second = jnp.int32(0)
        for j in reversed(range(migrate)):
            mine = source_ref[group * migrate + j] == my_group
            page = page_ref[group * migrate + j]
            second = jnp.where(mine, first, second)
            first = jnp.where(mine, page, first)
        return first, second

    pool_copy.wait()
    first, second = wanted_by(my_group)
    pages[own + my_group * CAP] = pool[first]
    pages[own + my_group * CAP + 1] = pool[second]
    for d in range(1, groups):
        to = lax.rem(my_group + d, groups)
        first, second = wanted_by(to)
        mig_out[d, 0] = pool[first]
        mig_out[d, 1] = pool[second]

    pl.semaphore_wait(barrier, groups + heads - 2)

    mig_copies = []
    for d in range(1, groups):
        to = lax.rem(my_group + d, groups)
        copy = pltpu.make_async_remote_copy(
            src_ref=mig_out.at[d],
            dst_ref=pages.at[pl.ds(own + my_group * CAP, CAP)],
            send_sem=mig_send.at[d],
            recv_sem=mig_recv.at[d],
            device_id=(to, me),
            device_id_type=MESH,
        )
        copy.start()
        mig_copies.append(copy)
    q_copies = []
    for d in range(1, heads):
        to = lax.rem(me + d, heads)
        copy = pltpu.make_async_remote_copy(
            src_ref=query_hbm.at[to],
            dst_ref=queries.at[me],
            send_sem=q_send.at[d],
            recv_sem=q_recv.at[d],
            device_id=(my_group, to),
            device_id_type=MESH,
        )
        copy.start()
        q_copies.append(copy)

    for j in range(migrate):
        from_group = source_ref[my_group * migrate + j]
        rank = jnp.int32(0)
        for i in range(j):
            rank = rank + jnp.where(source_ref[my_group * migrate + i] == from_group, 1, 0)
        place[j] = own + from_group * CAP + rank

    spare = keys.shape[0] - lanes
    pick = (
        lax.broadcasted_iota(jnp.int32, (spare, 2 * heads), 1)
        == lax.broadcasted_iota(jnp.int32, (spare, 2 * heads), 0) + 2 * me
    ) & (lax.broadcasted_iota(jnp.int32, (spare, 2 * heads), 0) < 2)
    keys[pl.ds(lanes, spare)] = jnp.dot(
        jnp.where(pick, 1.0, 0.0).astype(jnp.bfloat16),
        new_ref[...].reshape(2 * heads, lat),
        preferred_element_type=jnp.float32,
    ).astype(jnp.bfloat16)

    page_copy.wait()
    for copy in mig_copies:
        copy.wait_recv()

    def fill(seq, store):
        for k in range(slots):
            page = table_ref[seq * slots + k]
            moved = place[jnp.maximum(page - own, 0)]
            store(k, pages[jnp.where(page < own, page, moved)])

    kv_copies = []
    for d in range(1, heads):
        to = lax.rem(me + d, heads)

        def to_outgoing(k, value, d=d):
            kv_out[d, pl.ds(k * rows, rows)] = value

        fill(to, to_outgoing)
        copy = pltpu.make_async_remote_copy(
            src_ref=kv_out.at[d],
            dst_ref=keys.at[pl.ds(pl.multiple_of(me * width, width), width)],
            send_sem=kv_send.at[d],
            recv_sem=kv_recv.at[d],
            device_id=(my_group, to),
            device_id_type=MESH,
        )
        copy.start()
        kv_copies.append(copy)

    def to_keys(k, value):
        keys[pl.ds(pl.multiple_of(me * width + k * rows, rows), rows)] = value

    fill(me, to_keys)

    query_copy.wait()
    for copy in q_copies:
        copy.wait_recv()
    for copy in kv_copies:
        copy.wait_recv()

    row_count = heads * 2 * heads_each
    query = queries[...].reshape(row_count, lat)
    scale = (VD + ROPE) ** (-0.5)
    length = length_ref[me]
    chunk = min(256, lanes)
    starts = list(range(0, lanes, chunk))

    def dot_keys(start, size):
        return (
            lax.dot_general(
                query,
                keys[start : start + size],
                (((1,), (1,)), ((), ())),
                preferred_element_type=jnp.float32,
            )
            * scale
        )

    column = lax.broadcasted_iota(jnp.int32, (row_count, spare), 1)
    token = lax.broadcasted_iota(jnp.int32, (row_count, spare), 0) // heads_each % 2
    new_scores = jnp.where(column <= token, dot_keys(lanes, spare), HIDDEN)
    highest = jnp.max(new_scores, axis=1, keepdims=True)
    for start in starts:
        entry = lax.broadcasted_iota(jnp.int32, (1, chunk), 1) + start
        position = (
            entry // rows % slots * page_len + entry // width * rows + entry % rows
        )
        shown = jnp.where(position < length, dot_keys(start, chunk), HIDDEN)
        scores[:, start : start + chunk] = shown
        highest = jnp.maximum(highest, jnp.max(shown, axis=1, keepdims=True))
    weights = jnp.exp(new_scores - highest)
    totals = jnp.sum(weights, axis=1, keepdims=True)
    weighted = jnp.dot(
        weights.astype(jnp.bfloat16), keys[lanes:, :KVR], preferred_element_type=jnp.float32
    )
    for start in starts:
        weights = jnp.exp(scores[:, start : start + chunk] - highest)
        totals = totals + jnp.sum(weights, axis=1, keepdims=True)
        weighted = weighted + jnp.dot(
            weights.astype(jnp.bfloat16),
            keys[start : start + chunk, :KVR],
            preferred_element_type=jnp.float32,
        )
    lat_out[...] = (weighted / totals).astype(jnp.bfloat16).reshape(lat_out.shape)

    lat_copies = []
    for d in range(1, heads):
        to = lax.rem(me + d, heads)
        copy = pltpu.make_async_remote_copy(
            src_ref=lat_out.at[to],
            dst_ref=lat_in.at[me],
            send_sem=lat_send.at[d],
            recv_sem=lat_recv.at[d],
            device_id=(my_group, to),
            device_id_type=MESH,
        )
        copy.start()
        lat_copies.append(copy)
    lat_in[me] = lat_out[me]
    uv_copy.wait()
    for copy in lat_copies:
        copy.wait_recv()

    seq_tokens = 2 * heads
    target = lax.broadcasted_iota(jnp.int32, (row_count, row_count), 0)
    origin = lax.broadcasted_iota(jnp.int32, (row_count, row_count), 1)
    permute = jnp.where(
        origin == target % seq_tokens * heads_each + target // seq_tokens, 1.0, 0.0
    ).astype(jnp.bfloat16)
    by_head = jnp.dot(
        permute, lat_in[...].reshape(row_count, KVR), preferred_element_type=jnp.float32
    ).astype(jnp.bfloat16)
    for n in range(heads_each):
        values[me, :, n * VD : (n + 1) * VD] = jnp.dot(
            by_head[n * seq_tokens : (n + 1) * seq_tokens],
            w_uv[n],
            preferred_element_type=jnp.float32,
        ).astype(jnp.bfloat16)

    hv_copies = []
    for d in range(1, heads):
        to = lax.rem(me + d, heads)
        copy = pltpu.make_async_remote_copy(
            src_ref=values.at[me],
            dst_ref=values.at[me],
            send_sem=hv_send.at[d],
            recv_sem=hv_recv.at[d],
            device_id=(my_group, to),
            device_id_type=MESH,
        )
        copy.start()
        hv_copies.append(copy)
    out_copy.wait()
    depth = heads_each * VD

    def block(h):
        return jnp.dot(
            values[h],
            w_out[pl.ds(pl.multiple_of(h * depth, depth), depth)],
            preferred_element_type=jnp.float32,
        )

    result = block(me)
    for d in range(1, heads):
        hv_copies[d - 1].wait_recv()
        result = result + block(lax.rem(me - d + heads, heads))
    out_ref[...] = result.astype(out_ref.dtype)

    for copy in mig_copies + q_copies + kv_copies + lat_copies + hv_copies:
        copy.wait_send()


def shards(old_pool, mig_source, mig_page, page_table, lengths, queries, new_latent, w_uv, w_out):
    groups = lax.axis_size("group")
    heads = lax.axis_size("head")
    own, rows, lat = old_pool.shape
    seqs, tokens, heads_each, _ = queries.shape
    migrate = mig_source.shape[1]
    slots = page_table.shape[1] // seqs
    features = w_out.shape[1]
    dims = (groups, heads, own, slots, rows, migrate, heads_each, rows * heads)
    lanes = heads * slots * rows
    spare = 128
    half = jnp.bfloat16
    smem = pl.BlockSpec(memory_space=pltpu.SMEM)
    anywhere = pl.BlockSpec(memory_space=pl.ANY)
    vmem = pl.BlockSpec(memory_space=pltpu.VMEM)
    dma = pltpu.SemaphoreType.DMA
    result = pl.pallas_call(
        functools.partial(kernel, dims),
        out_shape=jax.ShapeDtypeStruct((seqs * tokens, features), half),
        in_specs=[smem, smem, smem, smem, anywhere, anywhere, vmem, anywhere, anywhere],
        out_specs=vmem,
        scratch_shapes=[
            pltpu.VMEM((own, rows, lat), half),
            pltpu.VMEM((own + groups * CAP, rows, lat), half),
            pltpu.VMEM((groups, CAP, rows, lat), half),
            pltpu.VMEM((lanes + spare, lat), half),
            pltpu.VMEM((heads, slots * rows, lat), half),
            pltpu.VMEM((heads, tokens * heads_each, lat), half),
            pltpu.VMEM((heads * tokens * heads_each, lanes), jnp.float32),
            pltpu.VMEM((heads, tokens * heads_each, KVR), half),
            pltpu.VMEM((heads, tokens * heads_each, KVR), half),
            pltpu.VMEM((heads, seqs * tokens, heads_each * VD), half),
            pltpu.VMEM(w_uv.shape, half),
            pltpu.VMEM(w_out.shape, half),
            pltpu.SMEM((migrate,), jnp.int32),
            dma((groups,)),
            dma((groups,)),
            dma((heads,)),
            dma((heads,)),
            dma((heads,)),
            dma((heads,)),
            dma((heads,)),
            dma((heads,)),
            dma((heads,)),
            dma((heads,)),
            dma((5,)),
        ],
        compiler_params=pltpu.CompilerParams(
            collective_id=0, has_side_effects=True, vmem_limit_bytes=48 * 1024 * 1024
        ),
    )(
        mig_source.reshape(-1),
        mig_page.reshape(-1),
        page_table.reshape(-1),
        lengths,
        old_pool,
        queries.reshape(seqs, tokens * heads_each, lat),
        new_latent,
        w_uv,
        w_out,
    )
    return result.reshape(seqs, tokens, features)


def solution(mesh):
    return jax.shard_map(
        shards,
        mesh=mesh,
        in_specs=(
            P("group", "head", None),
            P(),
            P(),
            P("group", None),
            P("group"),
            P("group", None, "head", None),
            P("group", None, None),
            P("head", None, None),
            P(None, "head"),
        ),
        out_specs=P("group", None, "head"),
        check_vma=False,
    )
```

time: 262 us -> 79.3 us (0.30)
  waiting for transfers between devices: 160 us -> 0 us
  Pallas kernels: 0 us -> 70.1 us
  other arithmetic: 28.8 us -> 1.37 us
  matrix products: 24.9 us -> 0 us
  local copies, waits for them, and re-layouts: 21.9 us -> 7.47 us
  between operations: 13.6 us -> 0.02 us
  starting transfers between devices: 11.8 us -> 0 us
    all_gather x2 -> x0, waiting for transfers between devices: 144 us -> none  [the longest x1 108 us: shards(): shard_rows = lax.all_gather(fresh_pool, 'head', axis=1, tiled=True)]
    pallas_call x0 -> x1, Pallas kernels: none -> 70.1 us  [shards(): pl.pallas_call(functools.partial(kernel, dims), out_shape=jax.ShapeDtypeS...]
    dot_general x6 -> x0, matrix products: 24.9 us -> none  [the longest x1 9.88 us: partial_attention(): jnp.einsum('sthc,slc->sthl', query, key_rows, preferred_element_type=jnp....]
    select_n x6 -> x0, other arithmetic: 20.2 us -> none  [the longest x2 18.4 us: shards(): jnp.take(shard_rows, page_map, axis=0)]
    gather x3 -> x0, local copies, waits for them, and re-layouts: 18.7 us -> none  [the longest x1 16.3 us: shards(): jnp.take(shard_rows, page_map, axis=0)]
    all_to_all x1 -> x0, waiting for transfers between devices: 16.2 us -> none  [shards(): lax.all_to_all(outgoing, 'group', split_axis=0, concat_axis=0, tiled=True)]
    all_to_all x1 -> x0, starting transfers between devices: 11.7 us -> none  [shards(): lax.all_to_all(outgoing, 'group', split_axis=0, concat_axis=0, tiled=True)]
    unnamed x10 -> x13, local copies, waits for them, and re-layouts: 1.18 us -> 6 us
  transfers between devices with their start and end apart: 3 -> 0, of which waited for: 3 -> 0; matrix products, arithmetic and copies ran while one was open for 3% -> 0% of each run, Pallas kernels for 0% -> 0%
where the time goes in v1:
time: 79.3 us; the launch traced here: 79 us
  Pallas kernels  70.1 us (88%)
  local copies, waits for them, and re-layouts  7.47 us (9%)
  other arithmetic  1.37 us (2%)
    pallas_call x1, Pallas kernels, shards(): pl.pallas_call(functools.partial(kernel, dims), out_shape=jax.ShapeDtypeS...  70.1 us
    unnamed x13, local copies, waits for them, and re-layouts  6 us

profile of v1, /device:TPU:1, one launch (start us, length us, event | category | flops | bytes accessed | tf_op | source)
XLA Modules:
  0.0 79.0 jit_solution(1909346638999848633)
XLA Ops:
  0.0 0.8 reshape.16.page_ref
  0.8 0.5 broadcast.3
  1.3 1.4 %reduce.3 = s32[16,16]{1,0:T(8,128)S(1)} reduce(s32[16,16,1]{1,2,0:T(1,128)} %param.10, s32[]{:T(128)} %broadcast.3), dimensions={2}, to_apply=%param.10.reduce_sub_computation.3 | reduce | bytes 2052 | tf_op args[1]
  2.7 0.1 reshape.15.source_ref
  2.7 0.0 copy-start
  2.7 1.2 %copy-done = bf16[8,512,128]{2,1,0:T(8,128)(2,1)S(1)} copy-done((bf16[8,512,128]{2,1,0:T(8,128)(2,1)S(1)}, bf16[8,512,128]{2,1,0:T(8,128)(2,1)}, u32[]{:S(2)}) %copy-start) | copy-done | bytes 1048600
  4.0 0.0 copy-start.1
  4.0 1.2 %copy-done.1 = bf16[48,16,576]{2,1,0:T(8,128)(2,1)S(1)} copy-done((bf16[48,16,576]{2,1,0:T(8,128)(2,1)S(1)}, bf16[48,16,576]{2,1,0:T(8,128)(2,1)}, u32[]{:S(2)}) %copy-start.1) | copy-done | bytes 884760
  5.2 0.0 copy-start.2
  5.2 1.0 %copy-done.2 = bf16[16,2,8,576]{3,2,1,0:T(8,128)(2,1)S(1)} copy-done((bf16[16,2,8,576]{3,2,1,0:T(8,128)(2,1)S(1)}, bf16[16,2,8,576]{3,2,1,0:T(8,128)(2,1)}, u32[]{:S(2)}) %copy-start.2) | copy-done | bytes 294936
  6.1 0.0 copy-start.3
  6.1 0.8 copy-done.3
  6.9 0.0 copy-start.4
  6.9 0.7 copy-done.4
  7.6 0.0 copy-start.5
  7.6 0.7 copy-done.5
  8.2 70.1 %shard_map.91 = bf16[32,256]{1,0:T(8,128)(2,1)S(1)} custom-call(s32[256]{0:T(256)S(1)} %reshape.15.source_ref, s32[256]{0:T(256)S(1)} %reshape.16.page_ref, s32[64]{0:T(128)S(1)} %bitcast.4, s32[16]{0:T(128)S(1)} %copy-done.5, bf16[48,16,576]{2,1,0:T(8,128)(2,1)S(1)} %copy-done.1, bf16[16,16,576]{2,1,0:T(8,128)(2,1)S(1)} %bitcast.3, ...), custom_call_target="tpu_custom_call" | custom-call | tf_op jit(solution)/shard_map/pallas_call | solution.py:317
  78.3 0.6 reshape.19
Async XLA Ops:
  2.7 1.2 %copy-start = (bf16[8,512,128]{2,1,0:T(8,128)(2,1)S(1)}, bf16[8,512,128]{2,1,0:T(8,128)(2,1)}, u32[]{:S(2)}) copy-start(bf16[8,512,128]{2,1,0:T(8,128)(2,1)} %w_uv_hbm.1) | copy-start | bytes 3145732
  4.0 1.2 %copy-start.1 = (bf16[48,16,576]{2,1,0:T(8,128)(2,1)S(1)}, bf16[48,16,576]{2,1,0:T(8,128)(2,1)}, u32[]{:S(2)}) copy-start(bf16[48,16,576]{2,1,0:T(8,128)(2,1)} %pool_hbm.1) | copy-start | bytes 2654212
  5.2 1.0 %copy-start.2 = (bf16[16,2,8,576]{3,2,1,0:T(8,128)(2,1)S(1)}, bf16[16,2,8,576]{3,2,1,0:T(8,128)(2,1)}, u32[]{:S(2)}) copy-start(bf16[16,2,8,576]{3,2,1,0:T(8,128)(2,1)} %param.14) | copy-start | bytes 884740
  6.1 0.8 copy-start.3
  6.9 0.7 copy-start.4
  7.6 0.7 copy-start.5

commit v2 on v0

v2 whole, which is shorter than its diff:
```python
import functools

import jax
import jax.numpy as jnp
from jax import lax
from jax.experimental import pallas as pl
from jax.experimental.pallas import tpu as pltpu
from jax.sharding import PartitionSpec as P

KVR = 512
ROPE = 64
VD = 128
CAP = 2
MESH = pl.DeviceIdType.MESH
HIDDEN = -1e30
CHUNKS = ((0, 128), (128, 128), (256, 128), (384, 128), (512, 64))


def kernel(
    dims,
    chunks,
    source_hbm,
    page_hbm,
    table_hbm,
    length_hbm,
    pool_hbm,
    query_hbm,
    new_hbm,
    w_uv_hbm,
    w_out_hbm,
    out_ref,
    source,
    page_of,
    table,
    length_of,
    place,
    new,
    new_keys,
    pool,
    queries,
    scores,
    lat_out,
    lat_in,
    values,
    w_uv,
    w_out,
    pages,
    mig_out,
    mig_in,
    keys,
    kv_out,
    kv_in,
    mig_send,
    mig_recv,
    q_send,
    q_recv,
    kv_send,
    kv_recv,
    lat_send,
    lat_recv,
    hv_send,
    hv_recv,
    local_sem,
):
    groups, heads, own, slots, rows, migrate, heads_each = dims
    my_group = lax.axis_index("group")
    me = lax.axis_index("head")
    columns = heads // 2
    part = lax.rem(me // 2, 2)
    column = me // 4 * 2 + lax.rem(me, 2)
    lat = pool_hbm.shape[2]
    width = slots * rows
    block_rows = 2 * width
    parts = range(len(chunks))
    last = len(chunks) - 1

    def device_of(col, half):
        return col // 2 * 4 + half * 2 + lax.rem(col, 2)

    barrier = pltpu.get_barrier_semaphore()
    for d in range(1, groups):
        to = lax.rem(my_group + d, groups)
        pl.semaphore_signal(barrier, inc=1, device_id=(to, me), device_id_type=MESH)
    for d in range(1, heads):
        to = lax.rem(me + d, heads)
        pl.semaphore_signal(barrier, inc=1, device_id=(my_group, to), device_id_type=MESH)

    def fetch(src, dst, n):
        copy = pltpu.make_async_copy(src, dst, local_sem.at[n])
        copy.start()
        return copy

    def remote(src, dst, send, recv, group, head):
        copy = pltpu.make_async_remote_copy(
            src_ref=src,
            dst_ref=dst,
            send_sem=send,
            recv_sem=recv,
            device_id=(group, head),
            device_id_type=MESH,
        )
        copy.start()
        return copy

    index_copies = [
        fetch(source_hbm, source, 0),
        fetch(page_hbm, page_of, 1),
        fetch(table_hbm, table, 2),
        fetch(length_hbm, length_of, 3),
    ]
    pool_copy = fetch(pool_hbm, pool, 4)
    new_copy = fetch(new_hbm, new, 5)
    query_copy = fetch(query_hbm.at[:, column], queries.at[me], 6)
    page_copies = [
        fetch(
            pool_hbm.at[:, :, pl.ds(start, size)], pages[c].at[pl.ds(0, own)], 9 + c
        )
        for c, (start, size) in enumerate(chunks)
    ]
    uv_copy = fetch(w_uv_hbm, w_uv, 7)
    out_copy = fetch(w_out_hbm, w_out, 8)

    def wanted_by(group):
        first = jnp.int32(0)
        second = jnp.int32(0)
        for j in reversed(range(migrate)):
            mine = source[group, 0, j] == my_group
            second = jnp.where(mine, first, second)
            first = jnp.where(mine, page_of[group, j], first)
        return first, second

    for copy in index_copies:
        copy.wait()
    pool_copy.wait()
    for d in range(groups):
        to = lax.rem(my_group + d, groups)
        first, second = (pool[page] for page in wanted_by(to))
        for c, (start, size) in enumerate(chunks[:last]):
            for r, value in enumerate((first, second)):
                cut = value[:, start : start + size]
                if d == 0:
                    pages[c][own + my_group * CAP + r] = cut
                else:
                    mig_out[c][d, r] = cut
        rotary = jnp.concatenate([first[:, KVR:], second[:, KVR:]], axis=1)
        if d == 0:
            mig_in[my_group] = rotary
        else:
            mig_out[last][d] = rotary

    pl.semaphore_wait(barrier, groups + heads - 2)

    def send_migration(c):
        copies = []
        for d in range(1, groups):
            to = lax.rem(my_group + d, groups)
            copies.append(
                remote(
                    mig_out[c].at[d],
                    pages[c].at[pl.ds(own + my_group * CAP, CAP)]
                    if c < last
                    else mig_in.at[my_group],
                    mig_send.at[c, d],
                    mig_recv.at[c, d],
                    to,
                    me,
                )
            )
        return copies

    def send_queries(half, first, n):
        copies = []
        for d in range(first, columns):
            col = lax.rem(column + d, columns)
            copies.append(
                remote(
                    query_hbm.at[:, col],
                    queries.at[me],
                    q_send.at[n, d],
                    q_recv.at[n, d],
                    my_group,
                    device_of(col, half),
                )
            )
        return copies

    mig_copies = [send_migration(0)]
    q_copies = send_queries(part, 1, 0)
    for c in parts[1:]:
        mig_copies.append(send_migration(c))

    for j in range(migrate):
        from_group = source[my_group, 0, j]
        rank = jnp.int32(0)
        for i in range(j):
            rank = rank + jnp.where(source[my_group, 0, i] == from_group, 1, 0)
        place[j] = own + from_group * CAP + rank

    new_copy.wait()
    spare = new_keys.shape[0]
    entry = lax.broadcasted_iota(jnp.int32, (spare, 2 * heads), 0)
    pick = (
        lax.broadcasted_iota(jnp.int32, (spare, 2 * heads), 1)
        == entry // 2 * heads + 2 * column + entry % 2
    ) & (entry < 4)
    new_keys[...] = jnp.dot(
        jnp.where(pick, 1.0, 0.0).astype(jnp.bfloat16),
        new[...].reshape(2 * heads, lat),
        preferred_element_type=jnp.float32,
    ).astype(jnp.bfloat16)

    def page_at(seq, k):
        page = table[0, seq * slots + k]
        return jnp.where(page < own, page, place[jnp.maximum(page - own, 0)])

    at = []
    for d in range(columns):
        col = lax.rem(column + d, columns)
        at.append([page_at(n // slots * columns + col, n % slots) for n in range(2 * slots)])

    kv_copies = []
    for c in parts:
        page_copies[c].wait()
        for copy in mig_copies[c]:
            copy.wait_recv()
        if c == last:
            for g in range(groups):
                for r in range(CAP):
                    pages[c][own + g * CAP + r] = mig_in[g, :, r * ROPE : (r + 1) * ROPE]

        def fill(block, d, c=c):
            if c < last:
                for n in range(2 * slots):
                    block[n * rows : (n + 1) * rows] = pages[c][at[d][n]]
                return
            for n in range(slots):
                k = n // 2 * slots + n % 2
                block[n * rows : (n + 1) * rows] = jnp.concatenate(
                    [pages[c][at[d][k]], pages[c][at[d][k + 2]]], axis=1
                )

        landing = keys[c] if c < last else kv_in
        copies = []
        for d in range(1, columns):
            fill(kv_out[c].at[d], d)
            copies.append(
                remote(
                    kv_out[c].at[d],
                    landing.at[column],
                    kv_send.at[c, d],
                    kv_recv.at[c, d],
                    my_group,
                    device_of(lax.rem(column + d, columns), part),
                )
            )
        fill(landing.at[column], 0)
        kv_copies.append(copies)
        if c == 1:
            q_copies = q_copies + send_queries(1 - part, 0, 1)

    row_count = heads * 2 * heads_each
    lanes = columns * width
    scale = (VD + ROPE) ** (-0.5)

    query_copy.wait()
    for copy in q_copies:
        copy.wait_recv()

    def dot_keys(s, start, size, key_rows):
        return lax.dot_general(
            queries[:, s, :, start : start + size].reshape(row_count, size),
            key_rows,
            (((1,), (1,)), ((), ())),
            preferred_element_type=jnp.float32,
        )

    def key_rows(c, s, size):
        return keys[c][:, s * width : (s + 1) * width, :size].reshape(lanes, size)

    for c, (start, size) in enumerate(chunks):
        for copy in kv_copies[c]:
            copy.wait_recv()
        if c == last:
            for col in range(columns):
                for n in range(4):
                    keys[c][col, n * 2 * rows : (n + 1) * 2 * rows] = kv_in[
                        col,
                        n // 2 * 2 * rows : (n // 2 + 1) * 2 * rows,
                        n % 2 * ROPE : (n % 2 + 1) * ROPE,
                    ]
        for s in range(2):
            some = dot_keys(s, start, size, key_rows(c, s, size))
            scores[s] = some if c == 0 else scores[s] + some

    number = lax.broadcasted_iota(jnp.int32, (1, lanes), 1)
    from_column = number // width
    position = (
        number // rows % slots * (rows * heads)
        + device_of(from_column, part) * rows
        + number % rows
    )
    new_column = lax.broadcasted_iota(jnp.int32, (row_count, spare), 1)
    token = lax.broadcasted_iota(jnp.int32, (row_count, spare), 0) // heads_each % 2
    stat_lane = lax.broadcasted_iota(jnp.int32, (row_count, 128), 1)

    def in_three(value):
        out = []
        for _ in range(3):
            top = value.astype(jnp.bfloat16).astype(jnp.float32)
            out.append(top)
            value = value - top
        return out

    mine_at = part * columns + column
    lat_copies = []
    for s in range(2):
        new_shown = (
            (new_column >= 2 * s) & (new_column - 2 * s <= token) & (new_column < 2 * s + 2)
        ) & (part == 0)
        new_scores = jnp.where(
            new_shown, dot_keys(s, 0, lat, new_keys[...]) * scale, HIDDEN
        )
        shown = jnp.where(position < length_of[s * columns + column], scores[s] * scale, HIDDEN)
        highest = jnp.maximum(
            jnp.max(new_scores, axis=1, keepdims=True), jnp.max(shown, axis=1, keepdims=True)
        )
        new_weights = jnp.exp(new_scores - highest)
        weights = jnp.exp(shown - highest)
        totals = jnp.sum(new_weights, axis=1, keepdims=True) + jnp.sum(
            weights, axis=1, keepdims=True
        )
        new_weights = new_weights.astype(jnp.bfloat16)
        weights = weights.astype(jnp.bfloat16)
        for c, (start, size) in enumerate(chunks):
            size = min(size, KVR - start)
            if size > 0:
                weighted = jnp.dot(
                    weights, key_rows(c, s, size), preferred_element_type=jnp.float32
                ) + jnp.dot(
                    new_weights,
                    new_keys[:, start : start + size],
                    preferred_element_type=jnp.float32,
                )
                lat_out[s, :, :, start : start + size] = (
                    (weighted / totals).astype(jnp.bfloat16).reshape(heads, -1, size)
                )
        stats = jnp.zeros((row_count, 128), jnp.float32)
        for n, piece in enumerate(in_three(highest) + in_three(totals)):
            stats = jnp.where(stat_lane == n, piece, stats)
        lat_out[s, :, :, KVR:] = stats.astype(jnp.bfloat16).reshape(heads, -1, 128)
        copies = []
        for d in range(1, heads):
            to = lax.rem(me + d, heads)
            copies.append(
                remote(
                    lat_out.at[s, to],
                    lat_in.at[s, mine_at],
                    lat_send.at[s, d],
                    lat_recv.at[s, d],
                    my_group,
                    to,
                )
            )
        lat_in[s, mine_at] = lat_out[s, me]
        lat_copies.append(copies)

    half_tokens = 2 * columns
    half_rows = half_tokens * heads_each
    target = lax.broadcasted_iota(jnp.int32, (half_rows, half_rows), 0)
    origin = lax.broadcasted_iota(jnp.int32, (half_rows, half_rows), 1)
    by_head = jnp.where(
        origin == target % half_tokens * heads_each + target // half_tokens, 1.0, 0.0
    ).astype(jnp.bfloat16)

    chips = heads // 2
    my_chip, core = me // 2, lax.rem(me, 2)
    sibling = my_chip * 2 + 1 - core

    def hand_on(s, h, to, n):
        return remote(
            values.at[s, h],
            values.at[s, h],
            hv_send.at[s, n],
            hv_recv.at[s, n],
            my_group,
            to,
        )

    uv_copy.wait()
    hv_copies = []
    passed = []
    for s in range(2):
        for copy in lat_copies[s]:
            copy.wait_recv()
        stat = []
        for z in range(2):
            tile = lat_in[s, z * columns : (z + 1) * columns, :, KVR:]
            stat.append(tile.reshape(half_rows, 128).astype(jnp.float32))

        def joined(z, n):
            return stat[z][:, n : n + 1] + stat[z][:, n + 1 : n + 2] + stat[z][:, n + 2 : n + 3]

        peaks = [joined(z, 0) for z in range(2)]
        top = jnp.maximum(peaks[0], peaks[1])
        shares = [joined(z, 3) * jnp.exp(peaks[z] - top) for z in range(2)]
        whole = shares[0] + shares[1]
        merged = sum(
            lat_in[s, z * columns : (z + 1) * columns, :, :KVR]
            .reshape(half_rows, KVR)
            .astype(jnp.float32)
            * (shares[z] / whole)
            for z in range(2)
        ).astype(jnp.bfloat16)
        sorted_rows = jnp.dot(by_head, merged, preferred_element_type=jnp.float32).astype(
            jnp.bfloat16
        )
        for n in range(heads_each):
            values[s, me, :, n * VD : (n + 1) * VD] = jnp.dot(
                sorted_rows[n * half_tokens : (n + 1) * half_tokens],
                w_uv[n],
                preferred_element_type=jnp.float32,
            ).astype(jnp.bfloat16)
        hv_copies.append(
            [
                hand_on(s, me, lax.rem(my_chip + d, chips) * 2 + core, d)
                for d in range(1, chips)
            ]
        )
        passed.append([hand_on(s, me, sibling, chips)])

    out_copy.wait()
    depth = heads_each * VD

    def block(h):
        return jnp.dot(
            values[:, h].reshape(2 * half_tokens, depth),
            w_out[pl.ds(pl.multiple_of(h * depth, depth), depth)],
            preferred_element_type=jnp.float32,
        )

    result = block(me)
    for s in range(2):
        for d in range(1, chips):
            origin_chip = lax.rem(my_chip - d + chips, chips)
            hv_copies[s][d - 1].wait_recv()
            passed[s].append(hand_on(s, origin_chip * 2 + core, sibling, chips + d))
            if s == 1:
                result = result + block(origin_chip * 2 + core)
    for d in range(chips):
        for s in range(2):
            passed[s][d].wait_recv()
        result = result + block(lax.rem(my_chip - d + chips, chips) * 2 + 1 - core)
    out_ref[...] = result.astype(out_ref.dtype)

    for copies in mig_copies + kv_copies + lat_copies + hv_copies + passed + [q_copies]:
        for copy in copies:
            copy.wait_send()


def shards(old_pool, mig_source, mig_page, page_table, lengths, queries, new_latent, w_uv, w_out):
    groups = lax.axis_size("group")
    heads = lax.axis_size("head")
    own, rows, lat = old_pool.shape
    seqs, tokens, heads_each, _ = queries.shape
    migrate = mig_source.shape[1]
    slots = page_table.shape[1] // seqs
    features = w_out.shape[1]
    dims = (groups, heads, own, slots, rows, migrate, heads_each)
    columns = heads // 2
    width = slots * rows
    lines = tokens * heads_each
    spare = 128
    half = jnp.bfloat16
    anywhere = pl.BlockSpec(memory_space=pl.ANY)
    dma = pltpu.SemaphoreType.DMA
    count = len(CHUNKS)
    result = pl.pallas_call(
        functools.partial(kernel, dims, CHUNKS),
        out_shape=jax.ShapeDtypeStruct((seqs * tokens, features), half),
        in_specs=[anywhere] * 9,
        out_specs=pl.BlockSpec(memory_space=pltpu.VMEM),
        scratch_shapes=[
            pltpu.SMEM((groups, 1, migrate), jnp.int32),
            pltpu.SMEM((groups, migrate), jnp.int32),
            pltpu.SMEM(page_table.shape, jnp.int32),
            pltpu.SMEM(lengths.shape, jnp.int32),
            pltpu.SMEM((migrate,), jnp.int32),
            pltpu.VMEM(new_latent.shape, half),
            pltpu.VMEM((spare, lat), half),
            pltpu.VMEM((own, rows, lat), half),
            pltpu.VMEM((heads, 2, lines, lat), half),
            pltpu.VMEM((2, heads * lines, columns * width), jnp.float32),
            pltpu.VMEM((2, heads, lines, KVR + 128), half),
            pltpu.VMEM((2, heads, lines, KVR + 128), half),
            pltpu.VMEM((2, heads, columns * tokens, heads_each * VD), half),
            pltpu.VMEM(w_uv.shape, half),
            pltpu.VMEM(w_out.shape, half),
            [pltpu.VMEM((own + groups * CAP, rows, size), half) for _, size in CHUNKS],
            [pltpu.VMEM((groups, CAP, rows, size), half) for _, size in CHUNKS[:-1]]
            + [pltpu.VMEM((groups, rows, CAP * ROPE), half)],
            pltpu.VMEM((groups, rows, CAP * ROPE), half),
            [pltpu.VMEM((columns, 2 * width, size), half) for _, size in CHUNKS],
            [pltpu.VMEM((columns, 2 * width, size), half) for _, size in CHUNKS[:-1]]
            + [pltpu.VMEM((columns, width, 2 * ROPE), half)],
            pltpu.VMEM((columns, width, 2 * ROPE), half),
            dma((count, groups)),
            dma((count, groups)),
            dma((2, columns)),
            dma((2, columns)),
            dma((count, columns)),
            dma((count, columns)),
            dma((2, heads)),
            dma((2, heads)),
            dma((2, heads)),
            dma((2, heads)),
            dma((9 + count,)),
        ],
        compiler_params=pltpu.CompilerParams(
            collective_id=0, has_side_effects=True, vmem_limit_bytes=62 * 1024 * 1024
        ),
    )(
        jnp.transpose(mig_source, (0, 2, 1)),
        mig_page,
        page_table,
        lengths,
        old_pool,
        queries.reshape(2, columns, lines, lat),
        new_latent,
        w_uv,
        w_out,
    )
    return result.reshape(seqs, tokens, features)


def solution(mesh):
    return jax.shard_map(
        shards,
        mesh=mesh,
        in_specs=(
            P("group", "head", None),
            P(),
            P(),
            P("group", None),
            P("group"),
            P("group", None, "head", None),
            P("group", None, None),
            P("head", None, None),
            P(None, "head"),
        ),
        out_specs=P("group", None, "head"),
        check_vma=False,
    )
```

time: 262 us -> 61.2 us (0.23)
  waiting for transfers between devices: 160 us -> 0 us
  Pallas kernels: 0 us -> 59.6 us
  other arithmetic: 28.8 us -> 0 us
  matrix products: 24.9 us -> 0 us
  local copies, waits for them, and re-layouts: 21.9 us -> 1.34 us
  between operations: 13.6 us -> 0.01 us
  starting transfers between devices: 11.8 us -> 0 us
    all_gather x2 -> x0, waiting for transfers between devices: 144 us -> none  [the longest x1 108 us: shards(): shard_rows = lax.all_gather(fresh_pool, 'head', axis=1, tiled=True)]
    pallas_call x0 -> x1, Pallas kernels: none -> 59.6 us  [shards(): pl.pallas_call(functools.partial(kernel, dims, CHUNKS), out_shape=jax.Sha...]
    dot_general x6 -> x0, matrix products: 24.9 us -> none  [the longest x1 9.88 us: partial_attention(): jnp.einsum('sthc,slc->sthl', query, key_rows, preferred_element_type=jnp....]
    select_n x6 -> x0, other arithmetic: 20.2 us -> none  [the longest x2 18.4 us: shards(): jnp.take(shard_rows, page_map, axis=0)]
    gather x3 -> x0, local copies, waits for them, and re-layouts: 18.7 us -> none  [the longest x1 16.3 us: shards(): jnp.take(shard_rows, page_map, axis=0)]
    all_to_all x1 -> x0, waiting for transfers between devices: 16.2 us -> none  [shards(): lax.all_to_all(outgoing, 'group', split_axis=0, concat_axis=0, tiled=True)]
    all_to_all x1 -> x0, starting transfers between devices: 11.7 us -> none  [shards(): lax.all_to_all(outgoing, 'group', split_axis=0, concat_axis=0, tiled=True)]
  transfers between devices with their start and end apart: 3 -> 0, of which waited for: 3 -> 0; matrix products, arithmetic and copies ran while one was open for 3% -> 0% of each run, Pallas kernels for 0% -> 0%
where the time goes in v2:
time: 61.2 us; the launch traced here: 61 us
  Pallas kernels  59.6 us (97%)
  local copies, waits for them, and re-layouts  1.34 us (2%)
    pallas_call x1, Pallas kernels, shards(): pl.pallas_call(functools.partial(kernel, dims, CHUNKS), out_shape=jax.Sha...  59.6 us
    reshape x1, local copies, waits for them, and re-layouts, shards(): return result.reshape(seqs, tokens, features)  1.34 us

profile of v2, /device:TPU:1, one launch (start us, length us, event | category | flops | bytes accessed | tf_op | source)
XLA Modules:
  0.0 61.0 jit_solution(11166524136766001570)
XLA Ops:
  0.0 59.6 %shard_map.91 = bf16[32,256]{1,0:T(8,128)(2,1)} custom-call(s32[16,1,16]{2,1,0:T(1,128)} %bitcast.3, s32[16,16]{1,0:T(8,128)} %page_hbm.1, s32[1,64]{1,0:T(1,128)} %table_hbm.1, s32[16]{0:T(128)} %length_hbm.1, bf16[48,16,576]{2,1,0:T(8,128)(2,1)} %pool_hbm.1, bf16[2,8,16,576]{3,2,1,0:T(8,128)(2,1)} %bitcast.2, bf16[16,2,576]{2,1,0:T(2,128)(2,1)} %new_hbm.1, ...), custom_call_target="tpu_custom_call" | custom-call | tf_op jit(solution)/shard_map/pallas_call | solution.py:477
  59.6 1.3 %reshape.7 = bf16[16,2,256]{2,1,0:T(2,128)(2,1)} reshape(bf16[32,256]{1,0:T(8,128)(2,1)} %shard_map.91) | data formatting | bytes 32768 | tf_op jit(solution)/shard_map/reshape | solution.py:532

commit v3 on v2

--- a/solution.py
+++ b/solution.py
@@ -13,6 +13,7 @@
 CAP = 2
 MESH = pl.DeviceIdType.MESH
 HIDDEN = -1e30
+PASS_AT = 2
 CHUNKS = ((0, 128), (128, 128), (256, 128), (384, 128), (512, 64))
 
 
@@ -74,16 +75,13 @@
     parts = range(len(chunks))
     last = len(chunks) - 1
 
+    mine_at = part * columns + column
+
     def device_of(col, half):
         return col // 2 * 4 + half * 2 + lax.rem(col, 2)
 
-    barrier = pltpu.get_barrier_semaphore()
-    for d in range(1, groups):
-        to = lax.rem(my_group + d, groups)
-        pl.semaphore_signal(barrier, inc=1, device_id=(to, me), device_id_type=MESH)
-    for d in range(1, heads):
-        to = lax.rem(me + d, heads)
-        pl.semaphore_signal(barrier, inc=1, device_id=(my_group, to), device_id_type=MESH)
+    def place_of(head):
+        return lax.rem(head // 2, 2) * columns + head // 4 * 2 + lax.rem(head, 2)
 
     def fetch(src, dst, n):
         copy = pltpu.make_async_copy(src, dst, local_sem.at[n])
@@ -102,6 +100,9 @@
         copy.start()
         return copy
 
+    def settle(ref, sem):
+        pltpu.make_async_copy(ref, ref, sem).wait()
+
     index_copies = [
         fetch(source_hbm, source, 0),
         fetch(page_hbm, page_of, 1),
@@ -109,8 +110,16 @@
         fetch(length_hbm, length_of, 3),
     ]
     pool_copy = fetch(pool_hbm, pool, 4)
+    barrier = pltpu.get_barrier_semaphore()
+    for d in range(1, groups):
+        to = lax.rem(my_group + d, groups)
+        pl.semaphore_signal(barrier, inc=1, device_id=(to, me), device_id_type=MESH)
+    for d in range(1, heads):
+        to = lax.rem(me + d, heads)
+        pl.semaphore_signal(barrier, inc=1, device_id=(my_group, to), device_id_type=MESH)
+
     new_copy = fetch(new_hbm, new, 5)
-    query_copy = fetch(query_hbm.at[:, column], queries.at[me], 6)
+    query_copy = fetch(query_hbm.at[:, column], queries.at[mine_at], 6)
     page_copies = [
         fetch(
             pool_hbm.at[:, :, pl.ds(start, size)], pages[c].at[pl.ds(0, own)], 9 + c
@@ -132,62 +141,68 @@
     for copy in index_copies:
         copy.wait()
     pool_copy.wait()
-    for d in range(groups):
-        to = lax.rem(my_group + d, groups)
-        first, second = (pool[page] for page in wanted_by(to))
-        for c, (start, size) in enumerate(chunks[:last]):
-            for r, value in enumerate((first, second)):
-                cut = value[:, start : start + size]
+    group_order = sorted(range(1, groups), key=lambda d: -min(d, groups - d))
+    picked = [wanted_by(lax.rem(my_group + d, groups)) for d in range(groups)]
+
+    def gather(c):
+        start, size = chunks[c]
+        for d in range(groups):
+            if c < last:
+                for r, page in enumerate(picked[d]):
+                    cut = pool[page, :, start : start + size]
+                    if d == 0:
+                        pages[c][own + my_group * CAP + r] = cut
+                    else:
+                        mig_out[c][d, r] = cut
+            else:
+                rotary = jnp.concatenate(
+                    [pool[page, :, start : start + size] for page in picked[d]], axis=1
+                )
                 if d == 0:
-                    pages[c][own + my_group * CAP + r] = cut
+                    mig_in[my_group] = rotary
                 else:
-                    mig_out[c][d, r] = cut
-        rotary = jnp.concatenate([first[:, KVR:], second[:, KVR:]], axis=1)
-        if d == 0:
-            mig_in[my_group] = rotary
-        else:
-            mig_out[last][d] = rotary
-
+                    mig_out[c][d] = rotary
+
+    def send_migration(c):
+        for d in group_order:
+            remote(
+                mig_out[c].at[d],
+                pages[c].at[pl.ds(own + my_group * CAP, CAP)]
+                if c < last
+                else mig_in.at[my_group],
+                mig_send.at[c],
+                mig_recv.at[c],
+                lax.rem(my_group + d, groups),
+                me,
+            )
+
+    column_order = sorted(range(1, columns), key=lambda d: -min(d, columns - d))
+
+    def send_queries():
+        for d in column_order:
+            col = lax.rem(column + d, columns)
+            remote(
+                query_hbm.at[:, col],
+                queries.at[mine_at],
+                q_send.at[0],
+                q_recv.at[0],
+                my_group,
+                device_of(col, part),
+            )
+
+    def pass_queries():
+        query_copy.wait()
+        settle(queries.at[pl.ds(0, columns - 1)], q_recv.at[0])
+        half = queries.at[pl.ds(pl.multiple_of(part * columns, columns), columns)]
+        remote(half, half, q_send.at[1], q_recv.at[1], my_group, device_of(column, 1 - part))
+
+    gather(0)
     pl.semaphore_wait(barrier, groups + heads - 2)
-
-    def send_migration(c):
-        copies = []
-        for d in range(1, groups):
-            to = lax.rem(my_group + d, groups)
-            copies.append(
-                remote(
-                    mig_out[c].at[d],
-                    pages[c].at[pl.ds(own + my_group * CAP, CAP)]
-                    if c < last
-                    else mig_in.at[my_group],
-                    mig_send.at[c, d],
-                    mig_recv.at[c, d],
-                    to,
-                    me,
-                )
-            )
-        return copies
-
-    def send_queries(half, first, n):
-        copies = []
-        for d in range(first, columns):
-            col = lax.rem(column + d, columns)
-            copies.append(
-                remote(
-                    query_hbm.at[:, col],
-                    queries.at[me],
-                    q_send.at[n, d],
-                    q_recv.at[n, d],
-                    my_group,
-                    device_of(col, half),
-                )
-            )
-        return copies
-
-    mig_copies = [send_migration(0)]
-    q_copies = send_queries(part, 1, 0)
+    send_migration(0)
+    send_queries()
     for c in parts[1:]:
-        mig_copies.append(send_migration(c))
+        gather(c)
+        send_migration(c)
 
     for j in range(migrate):
         from_group = source[my_group, 0, j]
@@ -218,11 +233,9 @@
         col = lax.rem(column + d, columns)
         at.append([page_at(n // slots * columns + col, n % slots) for n in range(2 * slots)])
 
-    kv_copies = []
     for c in parts:
         page_copies[c].wait()
-        for copy in mig_copies[c]:
-            copy.wait_recv()
+        settle(mig_out[c].at[pl.ds(1, groups - 1)], mig_recv.at[c])
         if c == last:
             for g in range(groups):
                 for r in range(CAP):
@@ -240,31 +253,30 @@
                 )
 
         landing = keys[c] if c < last else kv_in
-        copies = []
-        for d in range(1, columns):
+        for d in column_order:
             fill(kv_out[c].at[d], d)
-            copies.append(
-                remote(
-                    kv_out[c].at[d],
-                    landing.at[column],
-                    kv_send.at[c, d],
-                    kv_recv.at[c, d],
-                    my_group,
-                    device_of(lax.rem(column + d, columns), part),
-                )
+            remote(
+                kv_out[c].at[d],
+                landing.at[column],
+                kv_send.at[c],
+                kv_recv.at[c],
+                my_group,
+                device_of(lax.rem(column + d, columns), part),
             )
         fill(landing.at[column], 0)
-        kv_copies.append(copies)
-        if c == 1:
-            q_copies = q_copies + send_queries(1 - part, 0, 1)
+        if c == PASS_AT:
+            pass_queries()
+
+    for c in parts:
+        settle(mig_out[c].at[pl.ds(1, groups - 1)], mig_send.at[c])
 
     row_count = heads * 2 * heads_each
     lanes = columns * width
     scale = (VD + ROPE) ** (-0.5)
 
-    query_copy.wait()
-    for copy in q_copies:
-        copy.wait_recv()
+    settle(queries.at[pl.ds(0, columns - 1)], q_send.at[0])
+    settle(queries.at[pl.ds(0, columns)], q_send.at[1])
+    settle(queries.at[pl.ds(0, columns)], q_recv.at[1])
 
     def dot_keys(s, start, size, key_rows):
         return lax.dot_general(
@@ -278,8 +290,7 @@
         return keys[c][:, s * width : (s + 1) * width, :size].reshape(lanes, size)
 
     for c, (start, size) in enumerate(chunks):
-        for copy in kv_copies[c]:
-            copy.wait_recv()
+        settle(kv_out[c].at[pl.ds(1, columns - 1)], kv_recv.at[c])
         if c == last:
             for col in range(columns):
                 for n in range(4):
@@ -311,8 +322,9 @@
             value = value - top
         return out
 
-    mine_at = part * columns + column
-    lat_copies = []
+    head_order = sorted(range(1, heads), key=lambda d: -min(d, heads - d))
+    held = []
+    stats = jnp.zeros((row_count, 128), jnp.float32)
     for s in range(2):
         new_shown = (
             (new_column >= 2 * s) & (new_column - 2 * s <= token) & (new_column < 2 * s + 2)
@@ -320,7 +332,9 @@
         new_scores = jnp.where(
             new_shown, dot_keys(s, 0, lat, new_keys[...]) * scale, HIDDEN
         )
-        shown = jnp.where(position < length_of[s * columns + column], scores[s] * scale, HIDDEN)
+        shown = jnp.where(
+            position < length_of[s * columns + column], scores[s] * scale, HIDDEN
+        )
         highest = jnp.maximum(
             jnp.max(new_scores, axis=1, keepdims=True), jnp.max(shown, axis=1, keepdims=True)
         )
@@ -329,8 +343,14 @@
         totals = jnp.sum(new_weights, axis=1, keepdims=True) + jnp.sum(
             weights, axis=1, keepdims=True
         )
-        new_weights = new_weights.astype(jnp.bfloat16)
-        weights = weights.astype(jnp.bfloat16)
+        for n, piece in enumerate(in_three(highest) + in_three(totals)):
+            stats = jnp.where(stat_lane == 6 * s + n, piece, stats)
+        held.append(
+            (weights.astype(jnp.bfloat16), new_weights.astype(jnp.bfloat16), 1.0 / totals)
+        )
+    lat_out[0][:, :, KVR:] = stats.astype(jnp.bfloat16).reshape(heads, -1, 128)
+    for s in range(2):
+        weights, new_weights, share = held[s]
         for c, (start, size) in enumerate(chunks):
             size = min(size, KVR - start)
             if size > 0:
@@ -341,28 +361,22 @@
                     new_keys[:, start : start + size],
                     preferred_element_type=jnp.float32,
                 )
-                lat_out[s, :, :, start : start + size] = (
-                    (weighted / totals).astype(jnp.bfloat16).reshape(heads, -1, size)
+                lat_out[s][:, :, start : start + size] = (
+                    (weighted * share).astype(jnp.bfloat16).reshape(heads, -1, size)
                 )
-        stats = jnp.zeros((row_count, 128), jnp.float32)
-        for n, piece in enumerate(in_three(highest) + in_three(totals)):
-            stats = jnp.where(stat_lane == n, piece, stats)
-        lat_out[s, :, :, KVR:] = stats.astype(jnp.bfloat16).reshape(heads, -1, 128)
-        copies = []
-        for d in range(1, heads):
+        for d in head_order:
             to = lax.rem(me + d, heads)
-            copies.append(
-                remote(
-                    lat_out.at[s, to],
-                    lat_in.at[s, mine_at],
-                    lat_send.at[s, d],
-                    lat_recv.at[s, d],
-                    my_group,
-                    to,
-                )
+            remote(
+                lat_out[s].at[place_of(to)],
+                lat_in[s].at[mine_at],
+                lat_send.at[s],
+                lat_recv.at[s],
+                my_group,
+                to,
             )
-        lat_in[s, mine_at] = lat_out[s, me]
-        lat_copies.append(copies)
+        lat_in[s][mine_at] = lat_out[s][mine_at]
+    for c in parts:
+        settle(kv_out[c].at[pl.ds(1, columns - 1)], kv_send.at[c])
 
     half_tokens = 2 * columns
     half_rows = half_tokens * heads_each
@@ -380,7 +394,7 @@
         return remote(
             values.at[s, h],
             values.at[s, h],
-            hv_send.at[s, n],
+            hv_send.at[s],
             hv_recv.at[s, n],
             my_group,
             to,
@@ -390,22 +404,22 @@
     hv_copies = []
     passed = []
     for s in range(2):
-        for copy in lat_copies[s]:
-            copy.wait_recv()
-        stat = []
-        for z in range(2):
-            tile = lat_in[s, z * columns : (z + 1) * columns, :, KVR:]
-            stat.append(tile.reshape(half_rows, 128).astype(jnp.float32))
+        settle(lat_out[s].at[pl.ds(0, heads - 1)], lat_recv.at[s])
+        if s == 0:
+            stat = []
+            for z in range(2):
+                tile = lat_in[0][z * columns : (z + 1) * columns, :, KVR:]
+                stat.append(tile.reshape(half_rows, 128).astype(jnp.float32))
 
         def joined(z, n):
             return stat[z][:, n : n + 1] + stat[z][:, n + 1 : n + 2] + stat[z][:, n + 2 : n + 3]
 
-        peaks = [joined(z, 0) for z in range(2)]
+        peaks = [joined(z, 6 * s) for z in range(2)]
         top = jnp.maximum(peaks[0], peaks[1])
-        shares = [joined(z, 3) * jnp.exp(peaks[z] - top) for z in range(2)]
+        shares = [joined(z, 6 * s + 3) * jnp.exp(peaks[z] - top) for z in range(2)]
         whole = shares[0] + shares[1]
         merged = sum(
-            lat_in[s, z * columns : (z + 1) * columns, :, :KVR]
+            lat_in[s][z * columns : (z + 1) * columns, :, :KVR]
             .reshape(half_rows, KVR)
             .astype(jnp.float32)
             * (shares[z] / whole)
@@ -428,6 +442,8 @@
         )
         passed.append([hand_on(s, me, sibling, chips)])
 
+    for s in range(2):
+        settle(lat_out[s].at[pl.ds(0, heads - 1)], lat_send.at[s])
     out_copy.wait()
     depth = heads_each * VD
 
@@ -452,9 +468,8 @@
         result = result + block(lax.rem(my_chip - d + chips, chips) * 2 + 1 - core)
     out_ref[...] = result.astype(out_ref.dtype)
 
-    for copies in mig_copies + kv_copies + lat_copies + hv_copies + passed + [q_copies]:
-        for copy in copies:
-            copy.wait_send()
+    for s in range(2):
+        settle(values.at[s, pl.ds(0, 2 * chips - 1)], hv_send.at[s])
 
 
 def shards(old_pool, mig_source, mig_page, page_table, lengths, queries, new_latent, w_uv, w_out):
@@ -490,8 +505,8 @@
             pltpu.VMEM((own, rows, lat), half),
             pltpu.VMEM((heads, 2, lines, lat), half),
             pltpu.VMEM((2, heads * lines, columns * width), jnp.float32),
-            pltpu.VMEM((2, heads, lines, KVR + 128), half),
-            pltpu.VMEM((2, heads, lines, KVR + 128), half),
+            [pltpu.VMEM((heads, lines, size), half) for size in (KVR + 128, KVR)],
+            [pltpu.VMEM((heads, lines, size), half) for size in (KVR + 128, KVR)],
             pltpu.VMEM((2, heads, columns * tokens, heads_each * VD), half),
             pltpu.VMEM(w_uv.shape, half),
             pltpu.VMEM(w_out.shape, half),
@@ -503,15 +518,15 @@
             [pltpu.VMEM((columns, 2 * width, size), half) for _, size in CHUNKS[:-1]]
             + [pltpu.VMEM((columns, width, 2 * ROPE), half)],
             pltpu.VMEM((columns, width, 2 * ROPE), half),
-            dma((count, groups)),
-            dma((count, groups)),
-            dma((2, columns)),
-            dma((2, columns)),
-            dma((count, columns)),
-            dma((count, columns)),
-            dma((2, heads)),
-            dma((2, heads)),
-            dma((2, heads)),
+            dma((count,)),
+            dma((count,)),
+            dma((2,)),
+            dma((2,)),
+            dma((count,)),
+            dma((count,)),
+            dma((2,)),
+            dma((2,)),
+            dma((2,)),
             dma((2, heads)),
             dma((9 + count,)),
         ],

time: 61.2 us -> 56 us (0.915)
  Pallas kernels: 59.6 us -> 54.4 us
    pallas_call x1, Pallas kernels: 59.6 us -> 54.4 us  [shards(): pl.pallas_call(functools.partial(kernel, dims, CHUNKS), out_shape=jax.Sha...]
where the time goes in v3:
time: 56 us; the launch traced here: 55.8 us
  Pallas kernels  54.4 us (97%)
  local copies, waits for them, and re-layouts  1.34 us (2%)
    pallas_call x1, Pallas kernels, shards(): pl.pallas_call(functools.partial(kernel, dims, CHUNKS), out_shape=jax.Sha...  54.4 us
    reshape x1, local copies, waits for them, and re-layouts, shards(): return result.reshape(seqs, tokens, features)  1.34 us

profile of v3, /device:TPU:1, one launch (start us, length us, event | category | flops | bytes accessed | tf_op | source)
XLA Modules:
  0.0 55.8 jit_solution(4689781403300954163)
XLA Ops:
  0.0 54.4 %shard_map.91 = bf16[32,256]{1,0:T(8,128)(2,1)} custom-call(s32[16,1,16]{2,1,0:T(1,128)} %bitcast.3, s32[16,16]{1,0:T(8,128)} %page_hbm.1, s32[1,64]{1,0:T(1,128)} %table_hbm.1, s32[16]{0:T(128)} %length_hbm.1, bf16[48,16,576]{2,1,0:T(8,128)(2,1)} %pool_hbm.1, bf16[2,8,16,576]{3,2,1,0:T(8,128)(2,1)} %bitcast.2, bf16[16,2,576]{2,1,0:T(2,128)(2,1)} %new_hbm.1, ...), custom_call_target="tpu_custom_call" | custom-call | tf_op jit(solution)/shard_map/pallas_call | solution.py:492
  54.4 1.3 %reshape.7 = bf16[16,2,256]{2,1,0:T(2,128)(2,1)} reshape(bf16[32,256]{1,0:T(8,128)(2,1)} %shard_map.91) | data formatting | bytes 32768 | tf_op jit(solution)/shard_map/reshape | solution.py:547

commit v4 on v3

--- a/solution.py
+++ b/solution.py
@@ -38,6 +38,8 @@
     new,
     new_keys,
     pool,
+    q_raw,
+    q_out,
     queries,
     scores,
     lat_out,
@@ -80,9 +82,6 @@
     def device_of(col, half):
         return col // 2 * 4 + half * 2 + lax.rem(col, 2)
 
-    def place_of(head):
-        return lax.rem(head // 2, 2) * columns + head // 4 * 2 + lax.rem(head, 2)
-
     def fetch(src, dst, n):
         copy = pltpu.make_async_copy(src, dst, local_sem.at[n])
         copy.start()
@@ -119,7 +118,7 @@
         pl.semaphore_signal(barrier, inc=1, device_id=(my_group, to), device_id_type=MESH)
 
     new_copy = fetch(new_hbm, new, 5)
-    query_copy = fetch(query_hbm.at[:, column], queries.at[mine_at], 6)
+    query_copy = fetch(query_hbm, q_raw, 6)
     page_copies = [
         fetch(
             pool_hbm.at[:, :, pl.ds(start, size)], pages[c].at[pl.ds(0, own)], 9 + c
@@ -179,10 +178,18 @@
     column_order = sorted(range(1, columns), key=lambda d: -min(d, columns - d))
 
     def send_queries():
+        query_copy.wait()
+        for col in range(columns):
+            for s in range(2):
+                q_out[col, :, s * KVR : (s + 1) * KVR] = q_raw[s, col, :, :KVR]
+            q_out[col, :, 2 * KVR :] = jnp.concatenate(
+                [q_raw[s, col, :, KVR:] for s in range(2)], axis=1
+            )
+        queries[mine_at] = q_out[column]
         for d in column_order:
             col = lax.rem(column + d, columns)
             remote(
-                query_hbm.at[:, col],
+                q_out.at[col],
                 queries.at[mine_at],
                 q_send.at[0],
                 q_recv.at[0],
@@ -191,7 +198,6 @@
             )
 
     def pass_queries():
-        query_copy.wait()
         settle(queries.at[pl.ds(0, columns - 1)], q_recv.at[0])
         half = queries.at[pl.ds(pl.multiple_of(part * columns, columns), columns)]
         remote(half, half, q_send.at[1], q_recv.at[1], my_group, device_of(column, 1 - part))
@@ -279,8 +285,9 @@
     settle(queries.at[pl.ds(0, columns)], q_recv.at[1])
 
     def dot_keys(s, start, size, key_rows):
+        first = s * KVR + start if start < KVR else 2 * KVR + s * ROPE
         return lax.dot_general(
-            queries[:, s, :, start : start + size].reshape(row_count, size),
+            queries[:, :, first : first + size].reshape(row_count, size),
             key_rows,
             (((1,), (1,)), ((), ())),
             preferred_element_type=jnp.float32,
@@ -322,7 +329,6 @@
             value = value - top
         return out
 
-    head_order = sorted(range(1, heads), key=lambda d: -min(d, heads - d))
     held = []
     stats = jnp.zeros((row_count, 128), jnp.float32)
     for s in range(2):
@@ -330,7 +336,13 @@
             (new_column >= 2 * s) & (new_column - 2 * s <= token) & (new_column < 2 * s + 2)
         ) & (part == 0)
         new_scores = jnp.where(
-            new_shown, dot_keys(s, 0, lat, new_keys[...]) * scale, HIDDEN
+            new_shown,
+            (
+                dot_keys(s, 0, KVR, new_keys[:, :KVR])
+                + dot_keys(s, KVR, ROPE, new_keys[:, KVR:])
+            )
+            * scale,
+            HIDDEN,
         )
         shown = jnp.where(
             position < length_of[s * columns + column], scores[s] * scale, HIDDEN
@@ -364,16 +376,18 @@
                 lat_out[s][:, :, start : start + size] = (
                     (weighted * share).astype(jnp.bfloat16).reshape(heads, -1, size)
                 )
-        for d in head_order:
-            to = lax.rem(me + d, heads)
-            remote(
-                lat_out[s].at[place_of(to)],
-                lat_in[s].at[mine_at],
-                lat_send.at[s],
-                lat_recv.at[s],
-                my_group,
-                to,
-            )
+        for cross in (True, False):
+            half = 1 - part if cross else part
+            for d in column_order + [0] * cross:
+                col = lax.rem(column + d, columns)
+                remote(
+                    lat_out[s].at[half * columns + col],
+                    lat_in[s].at[mine_at],
+                    lat_send.at[s],
+                    lat_recv.at[s],
+                    my_group,
+                    device_of(col, half),
+                )
         lat_in[s][mine_at] = lat_out[s][mine_at]
     for c in parts:
         settle(kv_out[c].at[pl.ds(1, columns - 1)], kv_send.at[c])
@@ -486,7 +500,7 @@
     lines = tokens * heads_each
     spare = 128
     half = jnp.bfloat16
-    anywhere = pl.BlockSpec(memory_space=pl.ANY)
+    anywhere = pl.BlockSpec(memory_space=pltpu.HBM)
     dma = pltpu.SemaphoreType.DMA
     count = len(CHUNKS)
     result = pl.pallas_call(
@@ -503,7 +517,9 @@
             pltpu.VMEM(new_latent.shape, half),
             pltpu.VMEM((spare, lat), half),
             pltpu.VMEM((own, rows, lat), half),
-            pltpu.VMEM((heads, 2, lines, lat), half),
+            pltpu.VMEM((2, columns, lines, lat), half),
+            pltpu.VMEM((columns, lines, 2 * lat), half),
+            pltpu.VMEM((heads, lines, 2 * lat), half),
             pltpu.VMEM((2, heads * lines, columns * width), jnp.float32),
             [pltpu.VMEM((heads, lines, size), half) for size in (KVR + 128, KVR)],
             [pltpu.VMEM((heads, lines, size), half) for size in (KVR + 128, KVR)],
@@ -531,18 +547,23 @@
             dma((9 + count,)),
         ],
         compiler_params=pltpu.CompilerParams(
-            collective_id=0, has_side_effects=True, vmem_limit_bytes=62 * 1024 * 1024
+            collective_id=0, has_side_effects=True, vmem_limit_bytes=48 * 1024 * 1024
         ),
     )(
-        jnp.transpose(mig_source, (0, 2, 1)),
-        mig_page,
-        page_table,
-        lengths,
-        old_pool,
-        queries.reshape(2, columns, lines, lat),
-        new_latent,
-        w_uv,
-        w_out,
+        *(
+            pltpu.with_memory_space_constraint(operand, pltpu.HBM)
+            for operand in (
+                jnp.transpose(mig_source, (0, 2, 1)),
+                mig_page,
+                page_table,
+                lengths,
+                old_pool,
+                queries.reshape(2, columns, lines, lat),
+                new_latent,
+                w_uv,
+                w_out,
+            )
+        )
     )
     return result.reshape(seqs, tokens, features)
 

time: 56 us -> 54.5 us (0.973)
  local copies, waits for them, and re-layouts: 1.34 us -> 0.62 us
  Pallas kernels: 54.4 us -> 53.8 us
    reshape x1, local copies, waits for them, and re-layouts: 1.34 us -> 0.62 us  [shards(): return result.reshape(seqs, tokens, features)]
    pallas_call x1, Pallas kernels: 54.4 us -> 53.8 us  [shards(): pl.pallas_call(functools.partial(kernel, dims, CHUNKS), out_shape=jax.Sha...]
where the time goes in v4:
time: 54.5 us; the launch traced here: 54.4 us
  Pallas kernels  53.8 us (99%)
  local copies, waits for them, and re-layouts  0.62 us (1%)
    pallas_call x1, Pallas kernels, shards(): pl.pallas_call(functools.partial(kernel, dims, CHUNKS), out_shape=jax.Sha...  53.8 us

profile of v4, /device:TPU:1, one launch (start us, length us, event | category | flops | bytes accessed | tf_op | source)
XLA Modules:
  0.0 54.4 jit_solution(17264059472842492361)
XLA Ops:
  0.0 53.8 %shard_map.91 = bf16[32,256]{1,0:T(8,128)(2,1)S(1)} custom-call(s32[16,1,16]{2,1,0:T(1,128)} %bitcast.3, s32[16,16]{1,0:T(8,128)} %page_hbm.1, s32[1,64]{1,0:T(1,128)} %table_hbm.1, s32[16]{0:T(128)} %length_hbm.1, bf16[48,16,576]{2,1,0:T(8,128)(2,1)} %pool_hbm.1, bf16[2,8,16,576]{3,2,1,0:T(8,128)(2,1)} %bitcast.2, bf16[16,2,576]{2,1,0:T(2,128)(2,1)} %new_hbm.1, ...), custom_call_target="tpu_custom_call" | custom-call | tf_op jit(solution)/shard_map/pallas_call | solution.py:506
  53.8 0.6 %reshape.7 = bf16[16,2,256]{2,1,0:T(2,128)(2,1)} reshape(bf16[32,256]{1,0:T(8,128)(2,1)S(1)} %shard_map.91) | data formatting | bytes 32768 | tf_op jit(solution)/shard_map/reshape | solution.py:568

commit v5 on v4

--- a/solution.py
+++ b/solution.py
@@ -13,8 +13,8 @@
 CAP = 2
 MESH = pl.DeviceIdType.MESH
 HIDDEN = -1e30
-PASS_AT = 2
-CHUNKS = ((0, 128), (128, 128), (256, 128), (384, 128), (512, 64))
+PASS_AT = 1
+CHUNKS = ((0, 384), (384, 128), (512, 64))
 
 
 def kernel(
@@ -35,13 +35,13 @@
     table,
     length_of,
     place,
+    order,
     new,
     new_keys,
     pool,
     q_raw,
     q_out,
     queries,
-    scores,
     lat_out,
     lat_in,
     values,
@@ -51,12 +51,19 @@
     mig_out,
     mig_in,
     keys,
+    rotary_in,
+    rotary_keys,
+    seq_keys,
+    seq_rotary,
+    own_out,
+    own_rotary,
     kv_out,
-    kv_in,
     mig_send,
     mig_recv,
     q_send,
     q_recv,
+    own_send,
+    own_recv,
     kv_send,
     kv_recv,
     lat_send,
@@ -73,7 +80,7 @@
     column = me // 4 * 2 + lax.rem(me, 2)
     lat = pool_hbm.shape[2]
     width = slots * rows
-    block_rows = 2 * width
+    early = slots
     parts = range(len(chunks))
     last = len(chunks) - 1
 
@@ -180,11 +187,10 @@
     def send_queries():
         query_copy.wait()
         for col in range(columns):
+            pair = [q_raw[order[col]], q_raw[order[heads - 1 - col]]]
             for s in range(2):
-                q_out[col, :, s * KVR : (s + 1) * KVR] = q_raw[s, col, :, :KVR]
-            q_out[col, :, 2 * KVR :] = jnp.concatenate(
-                [q_raw[s, col, :, KVR:] for s in range(2)], axis=1
-            )
+                q_out[col, :, s * KVR : (s + 1) * KVR] = pair[s][:, :KVR]
+            q_out[col, :, 2 * KVR :] = jnp.concatenate([one[:, KVR:] for one in pair], axis=1)
         queries[mine_at] = q_out[column]
         for d in column_order:
             col = lax.rem(column + d, columns)
@@ -205,10 +211,8 @@
     gather(0)
     pl.semaphore_wait(barrier, groups + heads - 2)
     send_migration(0)
-    send_queries()
-    for c in parts[1:]:
-        gather(c)
-        send_migration(c)
+    gather(1)
+    send_migration(1)
 
     for j in range(migrate):
         from_group = source[my_group, 0, j]
@@ -217,12 +221,100 @@
             rank = rank + jnp.where(source[my_group, 0, i] == from_group, 1, 0)
         place[j] = own + from_group * CAP + rank
 
+    load = []
+    for i in range(heads):
+        moved = jnp.int32(0)
+        for k in range(slots):
+            moved = moved + jnp.where(table[0, i * slots + k] >= own, heads, 0)
+        load.append(moved - i)
+    ranks = [jnp.int32(0)] * heads
+    for i in range(heads):
+        for j in range(i):
+            ahead = jnp.where(load[j] > load[i], 1, 0)
+            ranks[i] = ranks[i] + ahead
+            ranks[j] = ranks[j] + 1 - ahead
+    for n in range(heads):
+        found = jnp.int32(0)
+        for i in range(heads):
+            found = found + jnp.where(ranks[i] == n, i, 0)
+        order[n] = found
+
+    at = []
+    home = []
+    for d in range(columns):
+        col = lax.rem(column + d, columns)
+        pair = (order[col], order[heads - 1 - col])
+        pages_of = [table[0, pair[n // slots] * slots + n % slots] for n in range(2 * slots)]
+        stays = [jnp.where(page < own, 1, 0) for page in pages_of]
+        behind = sum(stays)
+        ahead = jnp.int32(0)
+        spots = []
+        for n in range(2 * slots):
+            spots.append(jnp.where(pages_of[n] < own, ahead, behind + n - ahead))
+            ahead = ahead + stays[n]
+        if d == 0:
+            home = spots
+        wanted = [
+            jnp.where(page < own, page, place[jnp.maximum(page - own, 0)]) for page in pages_of
+        ]
+        at.append(
+            [
+                sum(jnp.where(spots[n] == p, wanted[n], 0) for n in range(2 * slots))
+                for p in range(2 * slots)
+            ]
+        )
+
+    def send_own():
+        for d in column_order + [0]:
+            cut = [pool[jnp.minimum(at[d][p], own - 1)] for p in range(early)]
+            pairs = [
+                jnp.concatenate([cut[i][:, KVR:], cut[i + 2][:, KVR:]], axis=1) for i in range(2)
+            ]
+            for p in range(early):
+                if d == 0:
+                    keys[column, p] = cut[p][:, :KVR]
+                else:
+                    own_out[d, p] = cut[p][:, :KVR]
+            for i in range(2):
+                if d == 0:
+                    rotary_in[0, column, i] = pairs[i]
+                else:
+                    own_rotary[d, i] = pairs[i]
+            if d > 0:
+                to = device_of(lax.rem(column + d, columns), part)
+                remote(
+                    own_out.at[d],
+                    keys.at[column, pl.ds(0, early)],
+                    own_send.at[0],
+                    own_recv.at[0],
+                    my_group,
+                    to,
+                )
+                remote(
+                    own_rotary.at[d],
+                    rotary_in.at[0, column],
+                    own_send.at[1],
+                    own_recv.at[1],
+                    my_group,
+                    to,
+                )
+
+    send_own()
+    for c in parts[2:]:
+        gather(c)
+        send_migration(c)
+        if c == 2:
+            send_queries()
+
     new_copy.wait()
     spare = new_keys.shape[0]
     entry = lax.broadcasted_iota(jnp.int32, (spare, 2 * heads), 0)
+    line = lax.broadcasted_iota(jnp.int32, (spare, 2 * heads), 1)
     pick = (
-        lax.broadcasted_iota(jnp.int32, (spare, 2 * heads), 1)
-        == entry // 2 * heads + 2 * column + entry % 2
+        line
+        == jnp.where(
+            entry < 2, 2 * order[column] + entry, 2 * order[heads - 1 - column] + entry - 2
+        )
     ) & (entry < 4)
     new_keys[...] = jnp.dot(
         jnp.where(pick, 1.0, 0.0).astype(jnp.bfloat16),
@@ -230,51 +322,42 @@
         preferred_element_type=jnp.float32,
     ).astype(jnp.bfloat16)
 
-    def page_at(seq, k):
-        page = table[0, seq * slots + k]
-        return jnp.where(page < own, page, place[jnp.maximum(page - own, 0)])
-
-    at = []
-    for d in range(columns):
-        col = lax.rem(column + d, columns)
-        at.append([page_at(n // slots * columns + col, n % slots) for n in range(2 * slots)])
-
-    for c in parts:
+    for c, (start, size) in enumerate(chunks):
         page_copies[c].wait()
         settle(mig_out[c].at[pl.ds(1, groups - 1)], mig_recv.at[c])
         if c == last:
             for g in range(groups):
                 for r in range(CAP):
                     pages[c][own + g * CAP + r] = mig_in[g, :, r * ROPE : (r + 1) * ROPE]
-
-        def fill(block, d, c=c):
-            if c < last:
-                for n in range(2 * slots):
-                    block[n * rows : (n + 1) * rows] = pages[c][at[d][n]]
-                return
-            for n in range(slots):
-                k = n // 2 * slots + n % 2
-                block[n * rows : (n + 1) * rows] = jnp.concatenate(
-                    [pages[c][at[d][k]], pages[c][at[d][k + 2]]], axis=1
+        for d in column_order + [0]:
+            cut = [pages[c][at[d][early + p]] for p in range(early)]
+            if c == last:
+                cut = [jnp.concatenate([cut[i], cut[i + 2]], axis=1) for i in range(2)]
+            for p, value in enumerate(cut):
+                if d > 0:
+                    kv_out[c][d, p] = value
+                elif c < last:
+                    keys[column, early + p, :, start : start + size] = value
+                else:
+                    rotary_in[1, column, p] = value
+            if d > 0:
+                remote(
+                    kv_out[c].at[d],
+                    keys.at[column, pl.ds(early, early), :, pl.ds(start, size)]
+                    if c < last
+                    else rotary_in.at[1, column],
+                    kv_send.at[c],
+                    kv_recv.at[c],
+                    my_group,
+                    device_of(lax.rem(column + d, columns), part),
                 )
-
-        landing = keys[c] if c < last else kv_in
-        for d in column_order:
-            fill(kv_out[c].at[d], d)
-            remote(
-                kv_out[c].at[d],
-                landing.at[column],
-                kv_send.at[c],
-                kv_recv.at[c],
-                my_group,
-                device_of(lax.rem(column + d, columns), part),
-            )
-        fill(landing.at[column], 0)
         if c == PASS_AT:
             pass_queries()
 
     for c in parts:
         settle(mig_out[c].at[pl.ds(1, groups - 1)], mig_send.at[c])
+    settle(own_out.at[pl.ds(1, columns - 1)], own_send.at[0])
+    settle(own_rotary.at[pl.ds(1, columns - 1)], own_send.at[1])
 
     row_count = heads * 2 * heads_each
     lanes = columns * width
@@ -293,28 +376,26 @@
             preferred_element_type=jnp.float32,
         )
 
-    def key_rows(c, s, size):
-        return keys[c][:, s * width : (s + 1) * width, :size].reshape(lanes, size)
-
-    for c, (start, size) in enumerate(chunks):
+    settle(own_out.at[pl.ds(1, columns - 1)], own_recv.at[0])
+    settle(own_rotary.at[pl.ds(1, columns - 1)], own_recv.at[1])
+    for c in parts:
         settle(kv_out[c].at[pl.ds(1, columns - 1)], kv_recv.at[c])
-        if c == last:
-            for col in range(columns):
-                for n in range(4):
-                    keys[c][col, n * 2 * rows : (n + 1) * 2 * rows] = kv_in[
-                        col,
-                        n // 2 * 2 * rows : (n // 2 + 1) * 2 * rows,
-                        n % 2 * ROPE : (n % 2 + 1) * ROPE,
-                    ]
-        for s in range(2):
-            some = dot_keys(s, start, size, key_rows(c, s, size))
-            scores[s] = some if c == 0 else scores[s] + some
+    for e in range(2):
+        for i in range(2):
+            rotary_keys[:, e * early + 2 * i : e * early + 2 * i + 2] = rotary_in[
+                e, :, :, :, i * ROPE : (i + 1) * ROPE
+            ]
+    page_lanes = columns * rows
+    for n in range(2 * slots):
+        s, k = n // slots, n % slots
+        here = pl.ds(k * page_lanes, page_lanes)
+        seq_keys[s, here] = keys[:, home[n]].reshape(page_lanes, KVR)
+        seq_rotary[s, here] = rotary_keys[:, home[n]].reshape(page_lanes, ROPE)
 
     number = lax.broadcasted_iota(jnp.int32, (1, lanes), 1)
-    from_column = number // width
     position = (
-        number // rows % slots * (rows * heads)
-        + device_of(from_column, part) * rows
+        number // page_lanes * (rows * heads)
+        + device_of(number // rows % columns, part) * rows
         + number % rows
     )
     new_column = lax.broadcasted_iota(jnp.int32, (row_count, spare), 1)
@@ -345,7 +426,9 @@
             HIDDEN,
         )
         shown = jnp.where(
-            position < length_of[s * columns + column], scores[s] * scale, HIDDEN
+            position < length_of[order[column if s == 0 else heads - 1 - column]],
+            (dot_keys(s, 0, KVR, seq_keys[s]) + dot_keys(s, KVR, ROPE, seq_rotary[s])) * scale,
+            HIDDEN,
         )
         highest = jnp.maximum(
             jnp.max(new_scores, axis=1, keepdims=True), jnp.max(shown, axis=1, keepdims=True)
@@ -363,19 +446,14 @@
     lat_out[0][:, :, KVR:] = stats.astype(jnp.bfloat16).reshape(heads, -1, 128)
     for s in range(2):
         weights, new_weights, share = held[s]
-        for c, (start, size) in enumerate(chunks):
-            size = min(size, KVR - start)
-            if size > 0:
-                weighted = jnp.dot(
-                    weights, key_rows(c, s, size), preferred_element_type=jnp.float32
-                ) + jnp.dot(
-                    new_weights,
-                    new_keys[:, start : start + size],
-                    preferred_element_type=jnp.float32,
-                )
-                lat_out[s][:, :, start : start + size] = (
-                    (weighted * share).astype(jnp.bfloat16).reshape(heads, -1, size)
-                )
+        for start in range(0, KVR, 256):
+            span = slice(start, start + 256)
+            weighted = jnp.dot(
+                weights, seq_keys[s, :, span], preferred_element_type=jnp.float32
+            ) + jnp.dot(new_weights, new_keys[:, span], preferred_element_type=jnp.float32)
+            lat_out[s][:, :, span] = (
+                (weighted * share).astype(jnp.bfloat16).reshape(heads, -1, 256)
+            )
         for cross in (True, False):
             half = 1 - part if cross else part
             for d in column_order + [0] * cross:
@@ -400,9 +478,19 @@
         origin == target % half_tokens * heads_each + target // half_tokens, 1.0, 0.0
     ).astype(jnp.bfloat16)
 
+    seat = lax.broadcasted_iota(jnp.int32, (2 * heads, 2 * heads), 1)
+    row = seat % 2
+    for n in range(heads):
+        seq = order[n if n < columns else heads - 1 - (n - columns)]
+        row = row + jnp.where(seat // 2 == n, 2 * seq, 0)
+    by_sequence = jnp.where(
+        lax.broadcasted_iota(jnp.int32, (2 * heads, 2 * heads), 0) == row, 1.0, 0.0
+    ).astype(jnp.bfloat16)
+
     chips = heads // 2
     my_chip, core = me // 2, lax.rem(me, 2)
     sibling = my_chip * 2 + 1 - core
+    chip_order = sorted(range(1, chips), key=lambda d: -min(d, chips - d))
 
     def hand_on(s, h, to, n):
         return remote(
@@ -451,7 +539,7 @@
         hv_copies.append(
             [
                 hand_on(s, me, lax.rem(my_chip + d, chips) * 2 + core, d)
-                for d in range(1, chips)
+                for d in chip_order
             ]
         )
         passed.append([hand_on(s, me, sibling, chips)])
@@ -470,17 +558,19 @@
 
     result = block(me)
     for s in range(2):
-        for d in range(1, chips):
+        for n, d in enumerate(chip_order):
             origin_chip = lax.rem(my_chip - d + chips, chips)
-            hv_copies[s][d - 1].wait_recv()
+            hv_copies[s][n].wait_recv()
             passed[s].append(hand_on(s, origin_chip * 2 + core, sibling, chips + d))
             if s == 1:
                 result = result + block(origin_chip * 2 + core)
-    for d in range(chips):
+    for k, d in enumerate([0] + chip_order):
         for s in range(2):
-            passed[s][d].wait_recv()
+            passed[s][k].wait_recv()
         result = result + block(lax.rem(my_chip - d + chips, chips) * 2 + 1 - core)
-    out_ref[...] = result.astype(out_ref.dtype)
+    out_ref[...] = jnp.dot(
+        by_sequence, result.astype(jnp.bfloat16), preferred_element_type=jnp.float32
+    ).astype(out_ref.dtype)
 
     for s in range(2):
         settle(values.at[s, pl.ds(0, 2 * chips - 1)], hv_send.at[s])
@@ -514,13 +604,13 @@
             pltpu.SMEM(page_table.shape, jnp.int32),
             pltpu.SMEM(lengths.shape, jnp.int32),
             pltpu.SMEM((migrate,), jnp.int32),
+            pltpu.SMEM((heads,), jnp.int32),
             pltpu.VMEM(new_latent.shape, half),
             pltpu.VMEM((spare, lat), half),
             pltpu.VMEM((own, rows, lat), half),
-            pltpu.VMEM((2, columns, lines, lat), half),
+            pltpu.VMEM((seqs, lines, lat), half),
             pltpu.VMEM((columns, lines, 2 * lat), half),
             pltpu.VMEM((heads, lines, 2 * lat), half),
-            pltpu.VMEM((2, heads * lines, columns * width), jnp.float32),
             [pltpu.VMEM((heads, lines, size), half) for size in (KVR + 128, KVR)],
             [pltpu.VMEM((heads, lines, size), half) for size in (KVR + 128, KVR)],
             pltpu.VMEM((2, heads, columns * tokens, heads_each * VD), half),
@@ -530,12 +620,19 @@
             [pltpu.VMEM((groups, CAP, rows, size), half) for _, size in CHUNKS[:-1]]
             + [pltpu.VMEM((groups, rows, CAP * ROPE), half)],
             pltpu.VMEM((groups, rows, CAP * ROPE), half),
-            [pltpu.VMEM((columns, 2 * width, size), half) for _, size in CHUNKS],
-            [pltpu.VMEM((columns, 2 * width, size), half) for _, size in CHUNKS[:-1]]
-            + [pltpu.VMEM((columns, width, 2 * ROPE), half)],
-            pltpu.VMEM((columns, width, 2 * ROPE), half),
+            pltpu.VMEM((columns, 2 * slots, rows, KVR), half),
+            pltpu.VMEM((2, columns, 2, rows, 2 * ROPE), half),
+            pltpu.VMEM((columns, 2 * slots, rows, ROPE), half),
+            pltpu.VMEM((2, columns * width, KVR), half),
+            pltpu.VMEM((2, columns * width, ROPE), half),
+            pltpu.VMEM((columns, slots, rows, KVR), half),
+            pltpu.VMEM((columns, 2, rows, 2 * ROPE), half),
+            [pltpu.VMEM((columns, slots, rows, size), half) for _, size in CHUNKS[:-1]]
+            + [pltpu.VMEM((columns, 2, rows, 2 * ROPE), half)],
             dma((count,)),
             dma((count,)),
+            dma((2,)),
+            dma((2,)),
             dma((2,)),
             dma((2,)),
             dma((count,)),
@@ -558,7 +655,7 @@
                 page_table,
                 lengths,
                 old_pool,
-                queries.reshape(2, columns, lines, lat),
+                queries.reshape(seqs, lines, lat),
                 new_latent,
                 w_uv,
                 w_out,

time: 54.5 us -> 53 us (0.972)
  Pallas kernels: 53.8 us -> 52.2 us
    pallas_call x1, Pallas kernels: 53.8 us -> 52.2 us  [shards(): pl.pallas_call(functools.partial(kernel, dims, CHUNKS), out_shape=jax.Sha...]
where the time goes in v5:
time: 53 us; the launch traced here: 52.9 us
  Pallas kernels  52.2 us (98%)
  local copies, waits for them, and re-layouts  0.62 us (1%)
    pallas_call x1, Pallas kernels, shards(): pl.pallas_call(functools.partial(kernel, dims, CHUNKS), out_shape=jax.Sha...  52.2 us

profile of v5, /device:TPU:1, one launch (start us, length us, event | category | flops | bytes accessed | tf_op | source)
XLA Modules:
  0.0 52.9 jit_solution(6273006776675906528)
XLA Ops:
  0.0 52.2 %shard_map.91 = bf16[32,256]{1,0:T(8,128)(2,1)S(1)} custom-call(s32[16,1,16]{2,1,0:T(1,128)} %bitcast.3, s32[16,16]{1,0:T(8,128)} %page_hbm.1, s32[1,64]{1,0:T(1,128)} %table_hbm.1, s32[16]{0:T(128)} %length_hbm.1, bf16[48,16,576]{2,1,0:T(8,128)(2,1)} %pool_hbm.1, bf16[16,16,576]{2,1,0:T(8,128)(2,1)} %bitcast.2, bf16[16,2,576]{2,1,0:T(2,128)(2,1)} %new_hbm.1, ...), custom_call_target="tpu_custom_call" | custom-call | tf_op jit(solution)/shard_map/pallas_call | solution.py:596
  52.3 0.6 %reshape.7 = bf16[16,2,256]{2,1,0:T(2,128)(2,1)} reshape(bf16[32,256]{1,0:T(8,128)(2,1)S(1)} %shard_map.91) | data formatting | bytes 32768 | tf_op jit(solution)/shard_map/reshape | solution.py:665

commit v6 on v5

--- a/solution.py
+++ b/solution.py
@@ -13,7 +13,7 @@
 CAP = 2
 MESH = pl.DeviceIdType.MESH
 HIDDEN = -1e30
-PASS_AT = 1
+PASS_AT = 0
 CHUNKS = ((0, 384), (384, 128), (512, 64))
 
 
@@ -109,6 +109,15 @@
     def settle(ref, sem):
         pltpu.make_async_copy(ref, ref, sem).wait()
 
+    group_order = sorted(range(1, groups), key=lambda d: -min(d, groups - d))
+    barrier = pltpu.get_barrier_semaphore()
+    for d in group_order:
+        to = lax.rem(my_group + d, groups)
+        pl.semaphore_signal(barrier, inc=1, device_id=(to, me), device_id_type=MESH)
+    for d in sorted(range(1, heads), key=lambda d: -min(d, heads - d)):
+        to = lax.rem(me + d, heads)
+        pl.semaphore_signal(barrier, inc=1, device_id=(my_group, to), device_id_type=MESH)
+
     index_copies = [
         fetch(source_hbm, source, 0),
         fetch(page_hbm, page_of, 1),
@@ -116,14 +125,6 @@
         fetch(length_hbm, length_of, 3),
     ]
     pool_copy = fetch(pool_hbm, pool, 4)
-    barrier = pltpu.get_barrier_semaphore()
-    for d in range(1, groups):
-        to = lax.rem(my_group + d, groups)
-        pl.semaphore_signal(barrier, inc=1, device_id=(to, me), device_id_type=MESH)
-    for d in range(1, heads):
-        to = lax.rem(me + d, heads)
-        pl.semaphore_signal(barrier, inc=1, device_id=(my_group, to), device_id_type=MESH)
-
     new_copy = fetch(new_hbm, new, 5)
     query_copy = fetch(query_hbm, q_raw, 6)
     page_copies = [
@@ -147,7 +148,6 @@
     for copy in index_copies:
         copy.wait()
     pool_copy.wait()
-    group_order = sorted(range(1, groups), key=lambda d: -min(d, groups - d))
     picked = [wanted_by(lax.rem(my_group + d, groups)) for d in range(groups)]
 
     def gather(c):
@@ -454,7 +454,7 @@
             lat_out[s][:, :, span] = (
                 (weighted * share).astype(jnp.bfloat16).reshape(heads, -1, 256)
             )
-        for cross in (True, False):
+        for cross in (False, True):
             half = 1 - part if cross else part
             for d in column_order + [0] * cross:
                 col = lax.rem(column + d, columns)

time: 53 us -> 52.8 us (level)
  no operation moved by 1% of the time
where the time goes in v6:
time: 52.8 us; the launch traced here: 52.7 us
  Pallas kernels  52.1 us (99%)
  local copies, waits for them, and re-layouts  0.62 us (1%)
    pallas_call x1, Pallas kernels, shards(): pl.pallas_call(functools.partial(kernel, dims, CHUNKS), out_shape=jax.Sha...  52.1 us

profile of v6, /device:TPU:1, one launch (start us, length us, event | category | flops | bytes accessed | tf_op | source)
XLA Modules:
  0.0 52.7 jit_solution(11469434934718444805)
XLA Ops:
  0.0 52.1 %shard_map.91 = bf16[32,256]{1,0:T(8,128)(2,1)S(1)} custom-call(s32[16,1,16]{2,1,0:T(1,128)} %bitcast.3, s32[16,16]{1,0:T(8,128)} %page_hbm.1, s32[1,64]{1,0:T(1,128)} %table_hbm.1, s32[16]{0:T(128)} %length_hbm.1, bf16[48,16,576]{2,1,0:T(8,128)(2,1)} %pool_hbm.1, bf16[16,16,576]{2,1,0:T(8,128)(2,1)} %bitcast.2, bf16[16,2,576]{2,1,0:T(2,128)(2,1)} %new_hbm.1, ...), custom_call_target="tpu_custom_call" | custom-call | tf_op jit(solution)/shard_map/pallas_call | solution.py:596
  52.1 0.6 %reshape.7 = bf16[16,2,256]{2,1,0:T(2,128)(2,1)} reshape(bf16[32,256]{1,0:T(8,128)(2,1)S(1)} %shard_map.91) | data formatting | bytes 32768 | tf_op jit(solution)/shard_map/reshape | solution.py:665
